TPU v7x, 128 devices: a whole 4x4x4 slice. The times are simulated.
128 devices in a mesh: readout: 16 (over y, x), pos: 8 (over z, core).
Axes of the slice: x: 4, y: 4, z: 4, core: 2. Of those that a mesh axis runs over, the one named last changes fastest.
Arguments:
- frames: float32 [128, 1024, 1024], P('pos', 'readout'), may hold values from 0 to 4
- dark: float32 [1024, 1024], P('readout'), may hold values from 0 to 0.5
- gain: float32 [1024, 1024], P('readout'), may hold values from 0.5 to 1.5
- offsets: int32 [128, 2], P('pos'), may hold values from 0 to 511
- object_field: float32 [2, 8192, 4096], P(None, 'readout', 'pos'), may hold values from -6 to 6
- probe: float32 [2, 512, 512], replicated, may hold values from -6 to 6
Outputs:
- object_new: float32 [2, 8192, 4096], P(None, 'readout', 'pos')
- probe_new: float32 [2, 512, 512], replicated
All inputs are finite; a program needn't handle non-finite values.
Results may differ from a plain program's by a relative error of at most 0.0003.
Values sent between devices are 32-bit elements; how exact they have to be, the bound alone decides.
No kernel may reach another device: no remote copies, remote signals or barrier semaphores. Data moves between devices by JAX's collectives and lax.ppermute only.
A program may use at most 576 MiB of HBM per device.

v0:
```python
import math

import jax
import jax.numpy as jnp
from jax import lax
from jax.sharding import PartitionSpec as P


def from_behind(block, axis, distance):
    devices = range(lax.axis_size(axis))
    route = [(i - distance, i) for i in devices if i - distance in devices]
    return lax.ppermute(block, axis, route)


def bin_pairs(stack_frames):
    frame_count, row_count, col_count = stack_frames.shape
    return stack_frames.reshape(frame_count, row_count // 2, 2, col_count // 2, 2).sum(axis=(2, 4))


def left_apply(tables, real_part, imag_part, direction):
    side = real_part.shape[2]
    joined = jnp.concatenate([real_part, imag_part], axis=2)
    mixed = jnp.einsum("tkn,bnm->btkm", tables, joined, precision=lax.Precision.HIGHEST)
    cos_real = mixed[:, 0, :, :side]
    cos_imag = mixed[:, 0, :, side:]
    sin_real = mixed[:, 1, :, :side]
    sin_imag = mixed[:, 1, :, side:]
    return (cos_real + direction * sin_imag, cos_imag - direction * sin_real)


def right_apply(wide_table, real_part, imag_part, direction):
    side = real_part.shape[1]
    joined = jnp.concatenate([real_part, imag_part], axis=1)
    mixed = jnp.einsum("bnm,mk->bnk", joined, wide_table, precision=lax.Precision.HIGHEST)
    cos_real = mixed[:, :side, :side]
    sin_real = mixed[:, :side, side:]
    cos_imag = mixed[:, side:, :side]
    sin_imag = mixed[:, side:, side:]
    return (cos_real + direction * sin_imag, cos_imag - direction * sin_real)


def transform_2d(tables, wide_table, real_part, imag_part, direction):
    mid_real, mid_imag = left_apply(tables, real_part, imag_part, direction)
    return right_apply(wide_table, mid_real, mid_imag, direction)


def on_device(frames, dark, gain, offsets, object_field, probe):
    stripe_index = lax.axis_index("readout")
    corrected = jnp.maximum(frames - dark, 0.0) * gain
    regrouped = lax.all_to_all(corrected, "readout", split_axis=0, concat_axis=1, tiled=True)
    binned = bin_pairs(regrouped)
    amplitude = jnp.sqrt(binned)
    owned_count = binned.shape[0]
    side = object_field.shape[1]
    my_offsets = lax.dynamic_slice_in_dim(offsets, stripe_index * owned_count, owned_count, 0)
    right_tile = from_behind(object_field, "pos", -1)
    wide_tiles = jnp.concatenate([object_field, right_tile], axis=2)
    below_tiles = from_behind(wide_tiles, "readout", -1)
    extended = jnp.concatenate([wide_tiles, below_tiles], axis=1)

    def take_patch(offset_pair):
        return lax.dynamic_slice(
            extended, (jnp.zeros((), jnp.int32), offset_pair[0], offset_pair[1]), (2, side, side)
        )

    patches = jax.vmap(take_patch)(my_offsets)
    obj_real = patches[:, 0]
    obj_imag = patches[:, 1]
    probe_real = probe[0]
    probe_imag = probe[1]
    wave_real = probe_real * obj_real - probe_imag * obj_imag
    wave_imag = probe_real * obj_imag + probe_imag * obj_real
    indices = jnp.arange(side, dtype=jnp.int32)
    product_mod = indices[:, None] * indices[None, :] % side
    angles = product_mod.astype(jnp.float32) * (2.0 * math.pi / side)
    norm_factor = 1.0 / math.sqrt(side)
    cosine = jnp.cos(angles) * norm_factor
    sine = jnp.sin(angles) * norm_factor
    tables = jnp.stack([cosine, sine])
    wide_table = jnp.concatenate([cosine, sine], axis=1)
    spec_real, spec_imag = transform_2d(tables, wide_table, wave_real, wave_imag, 1.0)
    magnitude = jnp.sqrt(spec_real * spec_real + spec_imag * spec_imag)
    factor = amplitude / jnp.maximum(magnitude, 0.25)
    back_real, back_imag = transform_2d(
        tables, wide_table, spec_real * factor, spec_imag * factor, -1.0
    )
    delta_real = back_real - wave_real
    delta_imag = back_imag - wave_imag
    grad_real = probe_real * delta_real + probe_imag * delta_imag
    grad_imag = probe_real * delta_imag - probe_imag * delta_real
    grad_pairs = jnp.stack([grad_real, grad_imag], axis=1)
    accum = jnp.zeros(extended.shape, jnp.float32)
    start = (jnp.zeros((), jnp.int32), my_offsets[0, 0], my_offsets[0, 1])
    accum = lax.dynamic_update_slice(accum, grad_pairs[0], start)
    lower_part = from_behind(accum[:, side:, :], "readout", 1)
    upper_part = accum[:, :side, :] + lower_part
    side_part = from_behind(upper_part[:, :, side:], "pos", 1)
    tile_grad = upper_part[:, :, :side] + side_part
    peak_power = jnp.max(probe_real * probe_real + probe_imag * probe_imag)
    object_new = object_field + tile_grad / peak_power
    probe_grad_real = jnp.sum(obj_real * delta_real + obj_imag * delta_imag, axis=0)
    probe_grad_imag = jnp.sum(obj_real * delta_imag - obj_imag * delta_real, axis=0)
    probe_grads = jnp.stack([probe_grad_real, probe_grad_imag])
    energy = jnp.sum(obj_real * obj_real + obj_imag * obj_imag, axis=0)
    grad_sum, energy_sum = lax.psum((probe_grads, energy), ("readout", "pos"))
    probe_new = probe + grad_sum / energy_sum
    return (object_new, probe_new)


def solution(mesh):
    in_specs = (
        P("pos", "readout", None),
        P("readout", None),
        P("readout", None),
        P("pos", None),
        P(None, "readout", "pos"),
        P(),
    )
    out_specs = (P(None, "readout", "pos"), P())
    return jax.shard_map(
        on_device, mesh=mesh, in_specs=in_specs, out_specs=out_specs, check_vma=False
    )
```

profile of v0, /device:TPU:1, one launch (start us, length us, event | category | flops | bytes accessed | tf_op | source)
XLA Modules:
  0.0 878.5 jit_solution(5660445275683505118)
XLA Ops:
  7.2 0.0 copy-start
  7.2 3.3 collective-permute-start
  10.5 0.0 copy-start.14
  10.5 0.0 copy-start.15
  10.5 3.2 constant_dynamic-update-slice_fusion.1
  13.7 22.7 %collective-permute-done = f32[2,512,512]{2,1,0:T(8,128)S(1)} collective-permute-done((f32[2,512,512]{2,1,0:T(8,128)}, f32[2,512,512]{2,1,0:T(8,128)S(1)}, u32[]{:S(2)}, u32[]{:S(2)}) %collective-permute-start) | collective-permute-done | bytes 2097184 | tf_op jit(solution)/shard_map/ppermute | solution.py:12
  36.4 1.5 constant_dynamic-update-slice_fusion
  38.0 1.3 collective-permute-start.1
  39.3 0.0 copy-done.14
  39.3 0.0 copy-done.15
  39.3 0.0 copy-done.10
  39.3 3.0 maximum_multiply_fusion
  42.3 9.4 %all-to-all-start = ((f32[16,64,1024]{2,1,0:T(8,128)}), f32[16,64,1024]{2,1,0:T(8,128)}, u32[]{:S(2)}, u32[]{:S(2)}) async-start(f32[16,64,1024]{2,1,0:T(8,128)} %maximum_multiply_fusion), calls=%async_computation | async-start | bytes 8388608 | tf_op jit(solution)/shard_map/all_to_all | solution.py:50
  51.7 0.0 all-reduce.3.cloned.1.call-start
  51.8 0.0 copy-done
  51.8 0.1 constant_dynamic-slice_fusion
  51.9 0.5 fusion.46
  60.1 5.0 sine_multiply_fusion.1
  65.2 5.0 sine_multiply_fusion
  70.2 84.4 %all-to-all-done = f32[16,64,1024]{2,1,0:T(8,128)} async-done(((f32[16,64,1024]{2,1,0:T(8,128)}), f32[16,64,1024]{2,1,0:T(8,128)}, u32[]{:S(2)}, u32[]{:S(2)}) %all-to-all-start) | async-done | bytes 4194336 | tf_op jit(solution)/shard_map/all_to_all | solution.py:50
  154.6 270.3 %reshape.232 = f32[512,2,512,2]{3,2,1,0:T(8,128)} reshape(f32[16,64,1024]{2,1,0:T(8,128)} %all-to-all-done) | data formatting | bytes 8388608 | tf_op jit(solution)/shard_map/reshape | solution.py:17
  424.9 81.0 %reduce_sum.8 = f32[512,512]{1,0:T(8,128)S(1)} reduce(f32[512,2,512,2]{3,2,1,0:T(8,128)} %reshape.232, f32[]{:T(128)} %constant.16.clone.1), dimensions={1,3}, to_apply=%region_0.0 | reduce | flops 786432 | bytes 5242884 | tf_op jit(solution)/shard_map/reduce_sum | solution.py:17
  505.9 0.3 copy.10
  506.3 0.0 collective-permute-done.1
  506.3 0.0 copy-start.3
  506.3 3.0 fusion.1
  509.3 0.0 copy-done.3
  509.3 0.0 copy-start.7
  509.4 0.0 copy-start.8
  509.4 0.5 fusion.28
  509.9 0.7 copy-done.7
  510.6 0.3 copy-done.8
  510.9 7.4 convolution_bitcast_fusion.3
  518.3 0.0 copy-start.11
  518.3 0.5 fusion.27
  518.8 0.7 copy-done.11
  519.5 0.3 copy-done.12
  519.8 7.6 convolution_bitcast_fusion.2
  527.4 0.8 fusion.33
  528.3 7.6 convolution_bitcast_fusion.1
  535.9 0.5 fusion.25
  536.4 7.3 convolution_bitcast_fusion
  543.7 2.1 fusion.30
  545.8 1.4 add_bitcast_fusion.1
  547.2 1.5 maximum_bitcast_fusion.8
  548.7 4.3 broadcast_in_dim.6
  553.0 15.1 %dynamic_update_slice.3 = f32[2,1024,1024]{2,1,0:T(8,128)} dynamic-update-slice(f32[2,1024,1024]{2,1,0:T(8,128)} %broadcast_in_dim.6, f32[2,512,512]{2,1,0:T(8,128)} %maximum_bitcast_fusion.8, s32[]{:T(128)} %constant.12.clone.1, s32[]{:T(128)S(6)} %select_n.44, s32[]{:T(128)S(6)} %select_n.45) | dynamic-update-slice | bytes 4194308 | tf_op jit(solution)/shard_map/dynamic_update_slice | solution.py:94
  568.1 2.7 slice.142
  570.8 8.9 %collective-permute-start.2 = (f32[2,512,1024]{2,1,0:T(8,128)S(1)}, f32[2,512,1024]{2,1,0:T(8,128)S(1)}, u32[]{:S(2)}, u32[]{:S(2)}) collective-permute-start(f32[2,512,1024]{2,1,0:T(8,128)S(1)} %slice.142), channel_id=1, source_target_pairs={{0,8},{8,16},{16,24},{24,32},{32,40},{40,48},{48,56},{56,64},{64,7... | collective-permute-start | bytes 12582920 | tf_op jit(solution)/shard_map/ppermute | solution.py:12
  579.7 1.2 add_bitcast_fusion
  580.9 69.0 %collective-permute-done.2 = f32[2,512,1024]{2,1,0:T(8,128)S(1)} collective-permute-done((f32[2,512,1024]{2,1,0:T(8,128)S(1)}, f32[2,512,1024]{2,1,0:T(8,128)S(1)}, u32[]{:S(2)}, u32[]{:S(2)}) %collective-permute-start.2) | collective-permute-done | bytes 4194336 | tf_op jit(solution)/shard_map/ppermute | solution.py:12
  649.9 0.0 copy-done.2
  649.9 1.4 slice_add_fusion
  651.3 1.5 slice.144
  652.8 1.1 copy-done.5
  653.9 42.8 %collective-permute-start.3 = (f32[2,512,512]{2,1,0:T(8,128)}, f32[2,512,512]{2,1,0:T(8,128)}, u32[]{:S(2)}, u32[]{:S(2)}) collective-permute-start(f32[2,512,512]{2,1,0:T(8,128)} %slice.144), channel_id=1, source_target_pairs={{0,1},{1,2},{2,3},{3,4},{4,5},{5,6},{6,7},{8,9},{9,10},{10,11},{11... | collective-permute-start | bytes 6291464 | tf_op jit(solution)/shard_map/ppermute | solution.py:12
  696.7 1.5 pad_maximum_fusion.2
  698.2 0.0 all-reduce.3.cloned.1.call-update
  698.2 164.8 %all-reduce.3.cloned.1.call-done = (f32[2,512,512]{2,1,0:T(8,128)}, f32[512,512]{1,0:T(8,128)}) async-done(((f32[2,512,512]{2,1,0:T(8,128)}, f32[512,512]{1,0:T(8,128)}), (f32[2,512,512]{2,1,0:T(8,128)}, f32[512,512]{1,0:T(8,128)})) %all-reduce.3.cloned.1.call-update) | async-done | bytes 3145744 | tf_op jit(solution)/shard_map/psum | solution.py:105
  863.0 4.0 divide_add_fusion
  867.0 0.0 collective-permute-done.3
  867.0 0.0 copy-done.6
  867.0 0.0 copy-start.1
  867.1 4.3 fusion.3
  (12 shorter events, 0.0 us)
Async XLA Ops:
  7.2 44.6 %copy-start = (s32[16,2]{0,1:T(2,128)S(1)}, s32[16,2]{0,1:T(2,128)}, u32[]{:S(2)}) copy-start(s32[16,2]{0,1:T(2,128)} %param.9) | copy-start | bytes 388
  7.2 29.3 %collective-permute-start = (f32[2,512,512]{2,1,0:T(8,128)}, f32[2,512,512]{2,1,0:T(8,128)S(1)}, u32[]{:S(2)}, u32[]{:S(2)}) collective-permute-start(f32[2,512,512]{2,1,0:T(8,128)} %param.10), channel_id=1, source_target_pairs={{1,0},{2,1},{3,2},{4,3},{5,4},{6,5},{7,6},{9,8},{10,9},{11,10},{12... | collective-permute-start | bytes 6291464 | tf_op jit(solution)/shard_map/ppermute | solution.py:12
  10.5 28.7 %copy-start.14 = (f32[64,1024]{1,0:T(8,128)S(1)}, f32[64,1024]{1,0:T(8,128)}, u32[]{:S(2)}) copy-start(f32[64,1024]{1,0:T(8,128)} %param.8) | copy-start | bytes 786436
  10.5 28.7 %copy-start.15 = (f32[64,1024]{1,0:T(8,128)S(1)}, f32[64,1024]{1,0:T(8,128)}, u32[]{:S(2)}) copy-start(f32[64,1024]{1,0:T(8,128)} %param.7) | copy-start | bytes 786436
  13.7 25.5 %copy-start.10 = (f32[16,64,1024]{2,1,0:T(8,128)S(1)}, f32[16,64,1024]{2,1,0:T(8,128)}, u32[]{:S(2)}) copy-start(f32[16,64,1024]{2,1,0:T(8,128)} %param.6) | copy-start | bytes 12582916
  38.0 468.3 %collective-permute-start.1 = (f32[2,512,1024]{2,1,0:T(8,128)}, f32[2,512,1024]{2,1,0:T(8,128)}, u32[]{:S(2)}, u32[]{:S(2)}) collective-permute-start(f32[2,512,1024]{2,1,0:T(8,128)} %constant_dynamic-update-slice_fusion), channel_id=1, source_target_pairs={{8,0},{16,8},{24,16},{32,24},{40,32},{48,40},{56,48},{64,56},{72,6... | collective-permute-start | bytes 12582920 | tf_op jit(solution)/shard_map/ppermute | solution.py:12
  42.3 112.3 %all-to-all-start = ((f32[16,64,1024]{2,1,0:T(8,128)}), f32[16,64,1024]{2,1,0:T(8,128)}, u32[]{:S(2)}, u32[]{:S(2)}) async-start(f32[16,64,1024]{2,1,0:T(8,128)} %maximum_multiply_fusion), calls=%async_computation | async-start | bytes 8388608 | tf_op jit(solution)/shard_map/all_to_all | solution.py:50
  51.7 811.3 %all-reduce.3.cloned.1.call-start = ((), (), s32[]{:S(2)}) async-start(), calls=%async_computation.1 | async-start | bytes 6291456 | tf_op jit(solution)/shard_map/psum | solution.py:105
  506.3 3.1 copy-start.3
  509.3 1.2 copy-start.7
  509.4 1.5 copy-start.8
  518.3 1.2 copy-start.11
  518.3 1.5 copy-start.12
  568.1 81.8 %copy-start.2 = (f32[2,1024,1024]{2,1,0:T(8,128)S(1)}, f32[2,1024,1024]{2,1,0:T(8,128)}, u32[]{:S(2)}) copy-start(f32[2,1024,1024]{2,1,0:T(8,128)} %dynamic_update_slice.3) | copy-start | bytes 25165828
  570.8 79.1 %collective-permute-start.2 = (f32[2,512,1024]{2,1,0:T(8,128)S(1)}, f32[2,512,1024]{2,1,0:T(8,128)S(1)}, u32[]{:S(2)}, u32[]{:S(2)}) collective-permute-start(f32[2,512,1024]{2,1,0:T(8,128)S(1)} %slice.142), channel_id=1, source_target_pairs={{0,8},{8,16},{16,24},{24,32},{32,40},{40,48},{48,56},{56,64},{64,7... | collective-permute-start | bytes 12582920 | tf_op jit(solution)/shard_map/ppermute | solution.py:12
  651.3 2.6 copy-start.5
  651.3 45.4 %copy-start.13 = (f32[1,512,512]{2,1,0:T(8,128)S(1)}, f32[1,512,512]{2,1,0:T(8,128)}, u32[]{:S(2)}) copy-start(f32[1,512,512]{2,1,0:T(8,128)} %get-tuple-element.15) | copy-start | bytes 3145732
  653.9 213.2 %collective-permute-start.3 = (f32[2,512,512]{2,1,0:T(8,128)}, f32[2,512,512]{2,1,0:T(8,128)}, u32[]{:S(2)}, u32[]{:S(2)}) collective-permute-start(f32[2,512,512]{2,1,0:T(8,128)} %slice.144), channel_id=1, source_target_pairs={{0,1},{1,2},{2,3},{3,4},{4,5},{5,6},{6,7},{8,9},{9,10},{10,11},{11... | collective-permute-start | bytes 6291464 | tf_op jit(solution)/shard_map/ppermute | solution.py:12
  698.2 164.8 %copy-start.4 = (f32[2,512,512]{2,1,0:T(8,128)S(1)}, f32[2,512,512]{2,1,0:T(8,128)}, u32[]{:S(2)}) copy-start(f32[2,512,512]{2,1,0:T(8,128)} %param.11) | copy-start | bytes 6291460
  863.0 4.0 copy-start.6
  863.0 4.0 copy-start.9
  867.0 4.3 copy-start.1
Sparse Core Ops, SparseCore 0:
  698.4 164.6 all-reduce.2
where the time goes:
time: 884 us; the launch traced here: 878 us
  waiting for transfers between devices  341 us (39%)
  local copies, waits for them, and re-layouts  303 us (34%)
  other arithmetic  117 us (13%)
  starting transfers between devices  65.8 us (7%)
  matrix products  29.9 us (3%)
  between operations  22.4 us (3%)
    reshape x1, local copies, waits for them, and re-layouts, bin_pairs(): stack_frames.reshape(frame_count, row_count // 2, 2, col_count // 2, 2)  270 us
    psum x1, waiting for transfers between devices, on_device(): grad_sum, energy_sum = lax.psum((probe_grads, energy), ('readout', 'pos'))  165 us
    ppermute x4, waiting for transfers between devices, from_behind(): return lax.ppermute(block, axis, route)  91.7 us
    all_to_all x1, waiting for transfers between devices, on_device(): lax.all_to_all(corrected, 'readout', split_axis=0, concat_axis=1, tiled=T...  84.4 us
    reduce_sum x1, other arithmetic, bin_pairs(): stack_frames.reshape(frame_count, row_count // 2, 2, col_count // 2, 2)  81 us
    ppermute x4, starting transfers between devices, from_behind(): return lax.ppermute(block, axis, route)  56.3 us
  transfers between devices with their start and end apart: 6, of which 4 were waited for; matrix products, arithmetic and copies ran while one was open for 43% of the time, Pallas kernels for 0%

commit v1 on v0

v1 whole, which is shorter than its diff:
```python
import functools
import math

import jax
import jax.numpy as jnp
import ml_dtypes
import numpy as np
from jax import lax
from jax.experimental import pallas as pl
from jax.experimental.pallas import tpu as pltpu
from jax.sharding import PartitionSpec as P

SIDE = 512
QUARTER = 128
ROWS = 16
COLS = 8
BOTH = ("readout", "pos")
F32 = jnp.float32
BF16 = jnp.bfloat16
VMEM_BYTES = 56 * 1024 * 1024


def split_table(table):
    high = table.astype(ml_dtypes.bfloat16)
    low = (table - high.astype(np.float64)).astype(ml_dtypes.bfloat16)
    return np.stack([high, low])


@functools.cache
def dft_tables():
    index = np.arange(QUARTER)
    tables = []
    for group in range(4):
        product_mod = (index[:, None] * (4 * index[None, :] + group)) % SIDE
        angles = product_mod * (2.0 * math.pi / SIDE)
        cosine = np.cos(angles) / math.sqrt(SIDE)
        sine = np.sin(angles) / math.sqrt(SIDE)
        tables.append(np.block([[cosine, -sine], [sine, cosine]]))
    straight = np.stack([split_table(table) for table in tables])
    turned = np.stack([split_table(table.T) for table in tables])
    return straight, turned


@functools.cache
def pair_table():
    table = np.zeros((2 * SIDE, SIDE), np.float32)
    for group in range(4):
        for place in range(QUARTER):
            for u in range(2):
                table[8 * place + 2 * group + u, group * QUARTER + place] = 1.0
    return table.astype(ml_dtypes.bfloat16)


def split_two(values):
    high = values.astype(BF16)
    low = (values - high.astype(F32)).astype(BF16)
    return high, low


def bin_kernel(scalars, frames, dark, gain, pairs, out, lanes, sums):
    step = pl.program_id(0)
    count = frames.shape[0]
    for n in range(count):
        corrected = jnp.maximum(frames[n] - dark[...], 0.0) * gain[...]
        for t in range(8):
            lanes[8 * n + t] = corrected[:, QUARTER * t : QUARTER * (t + 1)]
        for t in range(8):
            for group in range(4):
                total = lanes[8 * n + t, pl.ds(2 * group, 8, stride=8), :]
                total += lanes[8 * n + t, pl.ds(2 * group + 1, 8, stride=8), :]
                first = 32 * n + 8 * group
                sums[first : first + 8, QUARTER * t : QUARTER * (t + 1)] = total
    values = sums[...]
    high = values.astype(BF16)
    rest = values - high.astype(F32)
    mid = rest.astype(BF16)
    low = (rest - mid.astype(F32)).astype(BF16)
    table = pairs[...]
    binned = jnp.dot(low, table, preferred_element_type=F32)
    binned += jnp.dot(mid, table, preferred_element_type=F32)
    binned += jnp.dot(high, table, preferred_element_type=F32)
    for n in range(count):
        place = lax.rem(step * count + n + scalars[0], ROWS)
        out[place] = binned[32 * n : 32 * n + 32, :]


def bin_frames(flip, frames, dark, gain):
    per_step = 4
    return pl.pallas_call(
        bin_kernel,
        out_shape=jax.ShapeDtypeStruct((ROWS, 32, SIDE), F32),
        grid_spec=pltpu.PrefetchScalarGridSpec(
            num_scalar_prefetch=1,
            grid=(ROWS // per_step,),
            in_specs=[
                pl.BlockSpec((per_step, 64, 2 * SIDE), lambda s, f: (s, 0, 0)),
                pl.BlockSpec((64, 2 * SIDE), lambda s, f: (0, 0)),
                pl.BlockSpec((64, 2 * SIDE), lambda s, f: (0, 0)),
                pl.BlockSpec((2 * SIDE, SIDE), lambda s, f: (0, 0)),
            ],
            out_specs=pl.BlockSpec((ROWS, 32, SIDE), lambda s, f: (0, 0, 0)),
            scratch_shapes=[
                pltpu.VMEM((8 * per_step, 64, QUARTER), F32),
                pltpu.VMEM((32 * per_step, 2 * SIDE), F32),
            ],
        ),
        compiler_params=pltpu.CompilerParams(vmem_limit_bytes=VMEM_BYTES),
        cost_estimate=pl.CostEstimate(flops=2**31, bytes_accessed=6 * 2**20, transcendentals=0),
        name="bin_frames",
    )(flip, frames, dark, gain, jnp.asarray(pair_table()))


def roll_both(values, down, right):
    return pltpu.roll(pltpu.roll(values, down, 0), right, 1)


def roll_kernel(scalars, probe, out, peak):
    real = probe[0]
    imag = probe[1]
    peak[...] = jnp.broadcast_to(jnp.max(real * real + imag * imag, keepdims=True), (8, 128))
    out[0] = roll_both(real, scalars[0], scalars[1])
    out[1] = roll_both(imag, scalars[0], scalars[1])


def roll_probe(offset, probe):
    return pl.pallas_call(
        roll_kernel,
        out_shape=[jax.ShapeDtypeStruct((2, SIDE, SIDE), F32), jax.ShapeDtypeStruct((8, 128), F32)],
        in_specs=[pl.BlockSpec(memory_space=pltpu.SMEM), pl.BlockSpec(memory_space=pltpu.VMEM)],
        out_specs=[pl.BlockSpec(memory_space=pltpu.VMEM)] * 2,
        compiler_params=pltpu.CompilerParams(vmem_limit_bytes=VMEM_BYTES),
        cost_estimate=pl.CostEstimate(flops=2**22, bytes_accessed=4 * 2**20, transcendentals=0),
        name="roll_probe",
    )(offset, probe)


def times_i(pair):
    return -pair[1], pair[0]


def add(one, two):
    return one[0] + two[0], one[1] + two[1]


def sub(one, two):
    return one[0] - two[0], one[1] - two[1]


def butterfly(x0, x1, x2, x3, sign):
    even_sum, even_diff = add(x0, x2), sub(x0, x2)
    odd_sum, odd_diff = add(x1, x3), sub(x1, x3)
    turned = times_i(odd_diff)
    if sign < 0:
        first, third = sub(even_diff, turned), add(even_diff, turned)
    else:
        first, third = add(even_diff, turned), sub(even_diff, turned)
    return add(even_sum, odd_sum), first, sub(even_sum, odd_sum), third


def three_dots(left_high, left_low, right_high, right_low):
    total = jnp.dot(left_high, right_high, preferred_element_type=F32)
    total += jnp.dot(left_high, right_low, preferred_element_type=F32)
    total += jnp.dot(left_low, right_high, preferred_element_type=F32)
    return total


def main_kernel(
    scalars, tile, r0, r1, r2, r3, n0, n1, n2, n3, probe, binned, straight, turned, peak,
    away, kept, sum_away, sum_kept,
    patch, wave, wide, mid_high, mid_low, full,
):
    o0, o1, own_from, own_to, valid, core = (scalars[i] for i in range(6))
    quarters = [slice(QUARTER * a, QUARTER * (a + 1)) for a in range(4)]
    halves = [slice(0, QUARTER), slice(QUARTER, 2 * QUARTER)]
    rights = [r0, r1, r2, r3]
    others = [n0, n1, n2, n3]

    for a in range(4):
        rows = lax.broadcasted_iota(jnp.int32, (QUARTER, SIDE), 0) + QUARTER * a
        cols = lax.broadcasted_iota(jnp.int32, (QUARTER, SIDE), 1)
        own = (rows >= own_from) & (rows < own_to)
        here = cols >= o1
        for part in range(2):
            mine = jnp.where(here, tile[part, quarters[a], :], rights[a][part])
            mine = jnp.where(valid == 1, mine, 0.0)
            patch[part, quarters[a], :] = jnp.where(own, mine, others[a][part])
        obj = patch[0, quarters[a], :], patch[1, quarters[a], :]
        pr = probe[0, quarters[a], :], probe[1, quarters[a], :]
        wave[0, quarters[a], :] = pr[0] * obj[0] - pr[1] * obj[1]
        wave[1, quarters[a], :] = pr[0] * obj[1] + pr[1] * obj[0]
        blocks = [(wave[0, quarters[a], quarters[b]], wave[1, quarters[a], quarters[b]]) for b in range(4)]
        for g, pair in enumerate(butterfly(*blocks, -1)):
            for part in range(2):
                mid_high[g, quarters[a], halves[part]], mid_low[g, quarters[a], halves[part]] = split_two(pair[part])

    for g in range(4):
        out = three_dots(mid_high[g], mid_low[g], straight[g, 0], straight[g, 1])
        wide[0, :, quarters[g]] = out[:, :QUARTER]
        wide[1, :, quarters[g]] = out[:, QUARTER:]

    for b in range(4):
        blocks = [(wide[0, quarters[a], quarters[b]], wide[1, quarters[a], quarters[b]]) for a in range(4)]
        for h, pair in enumerate(butterfly(*blocks, -1)):
            for part in range(2):
                high, low = split_two(pair[part])
                full[h, 0, halves[part], quarters[b]] = high
                full[h, 1, halves[part], quarters[b]] = low

    for h in range(4):
        spec = three_dots(turned[h, 0], turned[h, 1], full[h, 0], full[h, 1])
        real, imag = spec[:QUARTER], spec[QUARTER:]
        power = real * real + imag * imag
        level = binned[:, 8 * h : 8 * h + 8, :].reshape(QUARTER, SIDE)
        factor = jnp.sqrt(level) * lax.rsqrt(jnp.maximum(power, 0.0625))
        for part, value in enumerate((real * factor, imag * factor)):
            high, low = split_two(value)
            full[h, 0, halves[part], :] = high
            full[h, 1, halves[part], :] = low

    for h in range(4):
        back = three_dots(straight[h, 0], straight[h, 1], full[h, 0], full[h, 1])
        wide[0, quarters[h], :] = back[:QUARTER]
        wide[1, quarters[h], :] = back[QUARTER:]

    for b in range(4):
        blocks = [(wide[0, quarters[h], quarters[b]], wide[1, quarters[h], quarters[b]]) for h in range(4)]
        for a, pair in enumerate(butterfly(*blocks, 1)):
            for part in range(2):
                mid_high[b, quarters[a], halves[part]], mid_low[b, quarters[a], halves[part]] = split_two(pair[part])

    for g in range(4):
        out = three_dots(mid_high[g], mid_low[g], turned[g, 0], turned[g, 1])
        wide[0, :, quarters[g]] = out[:, :QUARTER]
        wide[1, :, quarters[g]] = out[:, QUARTER:]

    scale = 1.0 / peak[0:1, 0:1]
    for a in range(4):
        rows = lax.broadcasted_iota(jnp.int32, (QUARTER, QUARTER), 0) + QUARTER * a
        own = (rows >= own_from) & (rows < own_to)
        keep = own & (valid == 1)
        blocks = [(wide[0, quarters[a], quarters[g]], wide[1, quarters[a], quarters[g]]) for g in range(4)]
        for b, back in enumerate(butterfly(*blocks, 1)):
            at = (quarters[a], quarters[b])
            dr = back[0] - wave[0, at[0], at[1]]
            di = back[1] - wave[1, at[0], at[1]]
            pr, pi = probe[0, at[0], at[1]], probe[1, at[0], at[1]]
            grad = (pr * dr + pi * di) * scale, (pr * di - pi * dr) * scale
            for part in range(2):
                kept[part, at[0], at[1]] = jnp.where(keep, grad[part], 0.0)
                away[part, at[0], at[1]] = jnp.where(own, 0.0, grad[part])
            cr, ci = patch[0, at[0], at[1]], patch[1, at[0], at[1]]
            wide[0, at[0], at[1]] = cr * dr + ci * di
            wide[1, at[0], at[1]] = cr * di - ci * dr
            wide[2, at[0], at[1]] = cr * cr + ci * ci

    up = lax.rem(SIDE - o0, SIDE)
    left = lax.rem(SIDE - o1, SIDE)
    half = SIDE // 2
    for part in range(3):
        wide[part] = roll_both(wide[part], up, left)
        sum_kept[part] = wide[part, pl.ds(pl.multiple_of(core * half, half), half), :]
        sum_away[part] = wide[part, pl.ds(pl.multiple_of((1 - core) * half, half), half), :]


def main_call(scalars, tile, rights, others, probe, binned, peak):
    straight, turned = dft_tables()
    whole = (2, SIDE, SIDE)
    half = (3, SIDE // 2, SIDE)
    vmem = pl.BlockSpec(memory_space=pltpu.VMEM)
    return pl.pallas_call(
        main_kernel,
        out_shape=[jax.ShapeDtypeStruct(s, F32) for s in (whole, whole, half, half)],
        in_specs=[pl.BlockSpec(memory_space=pltpu.SMEM)] + [vmem] * 14,
        out_specs=[vmem] * 4,
        scratch_shapes=[
            pltpu.VMEM(whole, F32),
            pltpu.VMEM(whole, F32),
            pltpu.VMEM((3, SIDE, SIDE), F32),
            pltpu.VMEM((4, SIDE, 2 * QUARTER), BF16),
            pltpu.VMEM((4, SIDE, 2 * QUARTER), BF16),
            pltpu.VMEM((4, 2, 2 * QUARTER, SIDE), BF16),
        ],
        compiler_params=pltpu.CompilerParams(vmem_limit_bytes=VMEM_BYTES),
        cost_estimate=pl.CostEstimate(flops=8 * 2**30, bytes_accessed=20 * 2**20, transcendentals=2**19),
        name="phase_update",
    )(scalars, tile, *rights, *others, probe, binned, jnp.asarray(straight), jnp.asarray(turned), peak)


def send(block, axis, route):
    return lax.ppermute(block, axis, route)


def device_pairs(move):
    pairs = []
    for r in range(ROWS):
        for p in range(COLS):
            target = move(r, p)
            if target is not None:
                pairs.append((r * COLS + p, target[0] * COLS + target[1]))
    return pairs


def gather_pairs(r, p):
    if p % 2 == 0:
        return (r - 1, p) if r > 0 else None
    return ((r + 1) % ROWS, p)


def scatter_pairs(r, p):
    if p % 2 == 0:
        return (r + 1, p) if r < ROWS - 1 else None
    return ((r - 1) % ROWS, p)


def ring_z(distance):
    return [(p, (p + 2 * distance) % COLS) for p in range(COLS)]


def ring_y(distance):
    return [(r, (r + 4 * distance) % ROWS) for r in range(ROWS)]


def ring_x(distance):
    return [(r, r // 4 * 4 + (r + distance) % 4) for r in range(ROWS)]


def scatter_sum(values, axis, ring, place):
    size = values.shape[1] // 4

    def piece(distance):
        start = lax.rem(place + distance, 4) * size
        return lax.dynamic_slice_in_dim(values, start, size, 1)

    parts = [send(piece(k), axis, ring(k)) for k in (2, 1, 3)]
    return (piece(0) + parts[0]) + (parts[1] + parts[2])


def gather_all(values, axis, ring, place):
    size = values.shape[1]
    parts = {k: send(values, axis, ring(k)) for k in (2, 1, 3)}
    out = jnp.zeros((values.shape[0], 4 * size, values.shape[2]), F32)
    out = lax.dynamic_update_slice_in_dim(out, values, place * size, 1)
    for k, part in parts.items():
        out = lax.dynamic_update_slice_in_dim(out, part, lax.rem(place - k + 4, 4) * size, 1)
    return out


def on_device(frames, dark, gain, offsets, object_field, probe):
    r = lax.axis_index("readout")
    p = lax.axis_index("pos")
    flip = lax.rem(p, 2)
    z = p // 2
    x, y = lax.rem(r, 4), r // 4
    position = lax.rem(r - flip + ROWS, ROWS)
    beside = lax.rem(r - 1 + flip + ROWS, ROWS)
    o0 = offsets[position, 0]
    o1 = offsets[position, 1]
    o1_beside = offsets[beside, 1]
    own_from = jnp.where(flip == 1, 0, o0)
    own_to = jnp.where(flip == 1, o0, SIDE)
    valid = jnp.where((flip == 1) & (r == 0), 0, 1)
    scalars = jnp.stack([o0, o1, own_from, own_to, valid, flip]).astype(jnp.int32)

    to_left = [(i, i - 1) for i in range(1, COLS)]
    to_right = [(i, i + 1) for i in range(COLS - 1)]
    chunks = [object_field[:, QUARTER * a : QUARTER * (a + 1)] for a in range(4)]
    rights = [send(chunk, "pos", to_left) for chunk in chunks]
    binned = bin_frames(flip[None].astype(jnp.int32), frames, dark, gain)
    regrouped = lax.all_to_all(binned, "readout", split_axis=0, concat_axis=0, tiled=True)
    cols = lax.broadcasted_iota(jnp.int32, (2, QUARTER, SIDE), 2)
    joined = [jnp.where(cols >= o1_beside, chunks[a], rights[a]) for a in range(4)]
    others = [send(block, BOTH, device_pairs(gather_pairs)) for block in joined]
    rolled, peak = roll_probe(scalars, probe)

    away, kept, sum_away, sum_kept = main_call(scalars, object_field, rights, others, rolled, regrouped, peak)

    swapped = send(sum_away, "pos", [(i, i ^ 1) for i in range(COLS)])
    arrived = [
        send(away[:, QUARTER * a : QUARTER * (a + 1)], BOTH, device_pairs(scatter_pairs)) for a in range(4)
    ]
    news = []
    for a in range(4):
        mine = kept[:, QUARTER * a : QUARTER * (a + 1)]
        outward = jnp.where(cols < o1, mine, 0.0) + jnp.where(cols < o1_beside, arrived[a], 0.0)
        landed = send(outward, "pos", to_right)
        inward = jnp.where(cols >= o1, mine, 0.0) + jnp.where(cols >= o1_beside, arrived[a], 0.0)
        news.append(chunks[a] + (inward + landed))
    object_new = jnp.concatenate(news, axis=1)

    total = sum_kept + swapped
    total = scatter_sum(total, "pos", ring_z, z)
    total = scatter_sum(total, "readout", ring_y, y)
    parts = [send(total, "readout", ring_x(k)) for k in (2, 1, 3)]
    total = (total + parts[0]) + (parts[1] + parts[2])
    start = flip * (SIDE // 2) + z * (SIDE // 8) + y * (SIDE // 32)
    own_probe = lax.dynamic_slice_in_dim(probe, start, SIDE // 32, 1)
    piece = own_probe + total[:2] / total[2:]
    piece = gather_all(piece, "readout", ring_y, y)
    piece = gather_all(piece, "pos", ring_z, z)
    other = send(piece, "pos", [(i, i ^ 1) for i in range(COLS)])
    first = jnp.where(flip == 0, piece, other)
    second = jnp.where(flip == 0, other, piece)
    probe_new = jnp.concatenate([first, second], axis=1)
    return (object_new, probe_new)


def solution(mesh):
    in_specs = (
        P("pos", "readout", None),
        P("readout", None),
        P("readout", None),
        P("pos", None),
        P(None, "readout", "pos"),
        P(),
    )
    out_specs = (P(None, "readout", "pos"), P())
    return jax.shard_map(
        on_device, mesh=mesh, in_specs=in_specs, out_specs=out_specs, check_vma=False
    )
```

time: 884 us -> 214 us (0.24)
  local copies, waits for them, and re-layouts: 303 us -> 8.56 us
  waiting for transfers between devices: 341 us -> 81.9 us
  other arithmetic: 117 us -> 19.4 us
  matrix products: 29.9 us -> 0 us
  Pallas kernels: 0 us -> 25.6 us
  between operations: 22.4 us -> 2.56 us
  starting transfers between devices: 65.8 us -> 75.2 us
    reshape x1 -> x0, local copies, waits for them, and re-layouts: 270 us -> none  [bin_pairs(): stack_frames.reshape(frame_count, row_count // 2, 2, col_count // 2, 2)]
    psum x1 -> x0, waiting for transfers between devices: 165 us -> none  [on_device(): grad_sum, energy_sum = lax.psum((probe_grads, energy), ('readout', 'pos'))]
    all_to_all x1, waiting for transfers between devices: 84.4 us -> 0.01 us  [on_device(): lax.all_to_all(binned, 'readout', split_axis=0, concat_axis=0, tiled=True)]
    reduce_sum x1 -> x0, other arithmetic: 81 us -> none  [bin_pairs(): stack_frames.reshape(frame_count, row_count // 2, 2, col_count // 2, 2)]
    dot_general x4 -> x0, matrix products: 29.9 us -> none  [the longest x2 15 us: left_apply(): jnp.einsum('tkn,bnm->btkm', tables, joined, precision=lax.Precision.HIGHEST)]
    pallas_call x0 -> x3, Pallas kernels: none -> 25.6 us  [the longest x1 14.1 us: main_call(): pl.pallas_call(main_kernel, out_shape=[jax.ShapeDtypeStruct(s, F32) for s...]
    dynamic_update_slice x1 -> x7, local copies, waits for them, and re-layouts: 15.1 us -> 0.13 us  [the longest x6 0.1 us: gather_all(): lax.dynamic_update_slice_in_dim(out, part, lax.rem(place - k + 4, 4) * si...]
    mul x4 -> x0, other arithmetic: 13.9 us -> none  [the longest x2 10.1 us: on_device(): sine = jnp.sin(angles) * norm_factor]
  transfers between devices with their start and end apart: 6 -> 34, of which waited for: 4 -> 15; matrix products, arithmetic and copies ran while one was open for 43% -> 9% of each run, Pallas kernels for 0% -> 5%
where the time goes in v1:
time: 214 us; the launch traced here: 213 us
  waiting for transfers between devices  81.9 us (38%)
  starting transfers between devices  75.2 us (35%)
  Pallas kernels  25.6 us (12%)
  other arithmetic  19.4 us (9%)
  local copies, waits for them, and re-layouts  8.56 us (4%)
  between operations  2.56 us (1%)
    ppermute x33, waiting for transfers between devices, send(): return lax.ppermute(block, axis, route)  81.9 us
    ppermute x33, starting transfers between devices, send(): return lax.ppermute(block, axis, route)  68.2 us
    pallas_call x1, Pallas kernels, main_call(): pl.pallas_call(main_kernel, out_shape=[jax.ShapeDtypeStruct(s, F32) for s...  14.1 us
    pallas_call x1, Pallas kernels, bin_frames(): pl.pallas_call(bin_kernel, out_shape=jax.ShapeDtypeStruct((ROWS, 32, SIDE...  7.1 us
    all_to_all x1, starting transfers between devices, on_device(): lax.all_to_all(binned, 'readout', split_axis=0, concat_axis=0, tiled=True)  6.97 us
    pallas_call x1, Pallas kernels, roll_probe(): pl.pallas_call(roll_kernel, out_shape=[jax.ShapeDtypeStruct((2, SIDE, SID...  4.36 us
  transfers between devices with their start and end apart: 34, of which 15 were waited for; matrix products, arithmetic and copies ran while one was open for 9% of the time, Pallas kernels for 5%

profile of v1, /device:TPU:1, one launch (start us, length us, event | category | flops | bytes accessed | tf_op | source)
XLA Modules:
  0.0 213.2 jit_solution(17827652881344907422)
XLA Ops:
  0.6 2.9 %fusion.3 = (f32[2,128,512]{2,1,0:T(8,128)}, f32[2,128,512]{2,1,0:T(8,128)}, f32[2,128,512]{2,1,0:T(8,128)}, f32[2,128,512]{2,1,0:T(8,128)}) fusion(f32[2,512,512]{2,1,0:T(8,128)} %tile.1), kind=kLoop, calls=%fused_computation.44 | loop fusion | bytes 4194304 | tf_op jit(solution)/shard_map/slice | solution.py:366
  3.5 3.3 %collective-permute-start = (f32[2,128,512]{2,1,0:T(8,128)}, f32[2,128,512]{2,1,0:T(8,128)}, u32[]{:S(2)}, u32[]{:S(2)}) collective-permute-start(f32[2,128,512]{2,1,0:T(8,128)} %get-tuple-element.37), channel_id=1, source_target_pairs={{1,0},{2,1},{3,2},{4,3},{5,4},{6,5},{7,6},{9,8},{10,9},{11,10},{12... | collective-permute-start | bytes 1572872 | tf_op jit(solution)/shard_map/ppermute | solution.py:290
  6.8 1.9 collective-permute-start.1
  8.8 1.9 collective-permute-start.2
  10.7 1.9 collective-permute-start.3
  12.6 7.1 %bin_frames.1 = f32[16,32,512]{2,1,0:T(8,128)} custom-call(s32[1]{0:T(128)} %bitcast.7.scalars, f32[16,64,1024]{2,1,0:T(8,128)} %frames.1, f32[64,1024]{1,0:T(8,128)} %dark.1, f32[64,1024]{1,0:T(8,128)} %gain.1, bf16[1024,512]{1,0:T(8,128)(2,1)} %constant.101.clone.pairs), custom_call_target="tpu_custom_call" | custom-call | flops 2147483648 | bytes 6291456 | tf_op jit(solution)/shard_map/bin_frames/pallas_call | solution.py:89
  19.7 7.0 %all-to-all-start = ((f32[16,32,512]{2,1,0:T(8,128)}), f32[16,32,512]{2,1,0:T(8,128)S(1)}, u32[]{:S(2)}, u32[]{:S(2)}) async-start(f32[16,32,512]{2,1,0:T(8,128)} %bin_frames.1), calls=%async_computation | async-start | bytes 2097152 | tf_op jit(solution)/shard_map/all_to_all | solution.py:369
  26.8 0.7 constant_dynamic-slice_fusion.7
  27.4 0.6 iota_compare_fusion.2
  28.1 4.6 %collective-permute-done.3.r3 = f32[2,128,512]{2,1,0:T(8,128)} collective-permute-done((f32[2,128,512]{2,1,0:T(8,128)}, f32[2,128,512]{2,1,0:T(8,128)}, u32[]{:S(2)}, u32[]{:S(2)}) %collective-permute-start.3) | collective-permute-done | bytes 524320 | tf_op jit(solution)/shard_map/ppermute | solution.py:290
  32.7 3.1 %broadcast_select_fusion.2 = (f32[2,128,512]{2,1,0:T(8,128)}, f32[2,128,512]{2,1,0:T(8,128)}, f32[2,128,512]{2,1,0:T(8,128)}, f32[2,128,512]{2,1,0:T(8,128)}) fusion(f32[2,128,512]{2,1,0:T(8,128)} %collective-permute-done.3.r3, pred[512]{0:T(512)(128)(4,1)S(1)} %iota_compare_fusion.2, f32[2,512,512]{2,1,0:T(8,128)S(1)} %copy-done, ...), kind=kLoop, calls=%fused_computation.13 | loop fusion | flops 524288 | bytes 6291968 | tf_op jit(solution)/shard_map/jit(_where)/select_n | solution.py:371
  35.8 2.9 %collective-permute-start.4 = (f32[2,128,512]{2,1,0:T(8,128)}, f32[2,128,512]{2,1,0:T(8,128)S(1)}, u32[]{:S(2)}, u32[]{:S(2)}) collective-permute-start(f32[2,128,512]{2,1,0:T(8,128)} %get-tuple-element.27), channel_id=1, source_target_pairs={{1,9},{3,11},{5,13},{7,15},{8,0},{9,17},{10,2},{11,19},{12,4},{13,... | collective-permute-start | bytes 1572872 | tf_op jit(solution)/shard_map/ppermute | solution.py:290
  38.7 3.3 %collective-permute-start.5 = (f32[2,128,512]{2,1,0:T(8,128)}, f32[2,128,512]{2,1,0:T(8,128)S(1)}, u32[]{:S(2)}, u32[]{:S(2)}) collective-permute-start(f32[2,128,512]{2,1,0:T(8,128)} %get-tuple-element.25), channel_id=1, source_target_pairs={{1,9},{3,11},{5,13},{7,15},{8,0},{9,17},{10,2},{11,19},{12,4},{13,... | collective-permute-start | bytes 1572872 | tf_op jit(solution)/shard_map/ppermute | solution.py:290
  42.0 2.8 %collective-permute-start.6 = (f32[2,128,512]{2,1,0:T(8,128)}, f32[2,128,512]{2,1,0:T(8,128)S(1)}, u32[]{:S(2)}, u32[]{:S(2)}) collective-permute-start(f32[2,128,512]{2,1,0:T(8,128)} %get-tuple-element.26), channel_id=1, source_target_pairs={{1,9},{3,11},{5,13},{7,15},{8,0},{9,17},{10,2},{11,19},{12,4},{13,... | collective-permute-start | bytes 1572872 | tf_op jit(solution)/shard_map/ppermute | solution.py:290
  44.8 3.3 %collective-permute-start.7 = (f32[2,128,512]{2,1,0:T(8,128)}, f32[2,128,512]{2,1,0:T(8,128)S(1)}, u32[]{:S(2)}, u32[]{:S(2)}) collective-permute-start(f32[2,128,512]{2,1,0:T(8,128)} %get-tuple-element.24), channel_id=1, source_target_pairs={{1,9},{3,11},{5,13},{7,15},{8,0},{9,17},{10,2},{11,19},{12,4},{13,... | collective-permute-start | bytes 1572872 | tf_op jit(solution)/shard_map/ppermute | solution.py:290
  49.5 1.9 stack.19.scalars
  51.4 4.4 %roll_probe.1 = (f32[2,512,512]{2,1,0:T(8,128)}, f32[8,128]{1,0:T(8,128)}) custom-call(s32[6]{0:T(128)} %stack.19.scalars, f32[2,512,512]{2,1,0:T(8,128)} %probe.1), custom_call_target="tpu_custom_call" | custom-call | flops 4194304 | bytes 4194304 | tf_op jit(solution)/shard_map/roll_probe/pallas_call | solution.py:126
  55.8 4.8 %collective-permute-done.6.n2 = f32[2,128,512]{2,1,0:T(8,128)S(1)} collective-permute-done((f32[2,128,512]{2,1,0:T(8,128)}, f32[2,128,512]{2,1,0:T(8,128)S(1)}, u32[]{:S(2)}, u32[]{:S(2)}) %collective-permute-start.6) | collective-permute-done | bytes 524320 | tf_op jit(solution)/shard_map/ppermute | solution.py:290
  60.6 5.6 %collective-permute-done.7.n3 = f32[2,128,512]{2,1,0:T(8,128)S(1)} collective-permute-done((f32[2,128,512]{2,1,0:T(8,128)}, f32[2,128,512]{2,1,0:T(8,128)S(1)}, u32[]{:S(2)}, u32[]{:S(2)}) %collective-permute-start.7) | collective-permute-done | bytes 524320 | tf_op jit(solution)/shard_map/ppermute | solution.py:290
  66.2 0.8 copy-done.12
  67.0 14.1 %phase_update.1 = (f32[2,512,512]{2,1,0:T(8,128)}, f32[2,512,512]{2,1,0:T(8,128)}, f32[3,256,512]{2,1,0:T(8,128)}, f32[3,256,512]{2,1,0:T(8,128)}) custom-call(s32[6]{0:T(128)} %stack.19.scalars, f32[2,512,512]{2,1,0:T(8,128)} %tile.1, f32[2,128,512]{2,1,0:T(8,128)} %collective-permute-done.r0, f32[2,128,512]{2,1,0:T(8,128)} %collective-permute-done.1.r1, ...), custom_call_target="tpu_custom_call" | custom-call | flops 8589934592 | bytes 20971520 | tf_op jit(solution)/shard_map/phase_update/pallas_call | solution.py:270
  81.2 3.6 %collective-permute-done.16 = f32[3,256,512]{2,1,0:T(8,128)S(1)} collective-permute-done((f32[3,256,512]{2,1,0:T(8,128)}, f32[3,256,512]{2,1,0:T(8,128)S(1)}, u32[]{:S(2)}, u32[]{:S(2)}) %collective-permute-start.16) | collective-permute-done | bytes 1572896 | tf_op jit(solution)/shard_map/ppermute | solution.py:290
  84.8 1.8 add.211
  86.6 4.1 %collective-permute-start.17 = (f32[3,64,512]{2,1,0:T(8,128)S(1)}, f32[3,64,512]{2,1,0:T(8,128)S(1)}, u32[]{:S(2)}, u32[]{:S(2)}) collective-permute-start(f32[3,64,512]{2,1,0:T(8,128)S(1)} %get-tuple-element.38), channel_id=1, source_target_pairs={{0,4},{1,5},{2,6},{3,7},{4,0},{5,1},{6,2},{7,3},{8,12},{9,13},{10,... | collective-permute-start | bytes 1179656 | tf_op jit(solution)/shard_map/ppermute | solution.py:290
  90.7 2.3 %collective-permute-start.18 = (f32[3,64,512]{2,1,0:T(8,128)S(1)}, f32[3,64,512]{2,1,0:T(8,128)S(1)}, u32[]{:S(2)}, u32[]{:S(2)}) collective-permute-start(f32[3,64,512]{2,1,0:T(8,128)S(1)} %get-tuple-element.40), channel_id=1, source_target_pairs={{0,2},{1,3},{2,4},{3,5},{4,6},{5,7},{6,0},{7,1},{8,10},{9,11},{10,... | collective-permute-start | bytes 1179656 | tf_op jit(solution)/shard_map/ppermute | solution.py:290
  93.1 0.4 collective-permute-start.19
  93.4 6.7 %collective-permute-done.17 = f32[3,64,512]{2,1,0:T(8,128)S(1)} collective-permute-done((f32[3,64,512]{2,1,0:T(8,128)S(1)}, f32[3,64,512]{2,1,0:T(8,128)S(1)}, u32[]{:S(2)}, u32[]{:S(2)}) %collective-permute-start.17) | collective-permute-done | bytes 393248 | tf_op jit(solution)/shard_map/ppermute | solution.py:290
  100.1 8.6 %collective-permute-done.18 = f32[3,64,512]{2,1,0:T(8,128)S(1)} collective-permute-done((f32[3,64,512]{2,1,0:T(8,128)S(1)}, f32[3,64,512]{2,1,0:T(8,128)S(1)}, u32[]{:S(2)}, u32[]{:S(2)}) %collective-permute-start.18) | collective-permute-done | bytes 393248 | tf_op jit(solution)/shard_map/ppermute | solution.py:290
  108.8 2.0 collective-permute-done.19
  110.7 1.1 add_add_fusion.4
  111.9 0.9 collective-permute-start.20
  112.8 0.2 collective-permute-start.21
  113.0 2.5 %collective-permute-start.22 = (f32[3,16,512]{2,1,0:T(8,128)S(1)}, f32[3,16,512]{2,1,0:T(8,128)S(1)}, u32[]{:S(2)}, u32[]{:S(2)}) collective-permute-start(f32[3,16,512]{2,1,0:T(8,128)S(1)} %get-tuple-element.42), channel_id=1, source_target_pairs={{0,96},{8,104},{16,112},{24,120},{32,0},{40,8},{48,16},{56,24},{64... | collective-permute-start | bytes 294920 | tf_op jit(solution)/shard_map/ppermute | solution.py:290
  115.5 1.8 collective-permute-done.20
  117.3 2.6 %collective-permute-done.21 = f32[3,16,512]{2,1,0:T(8,128)S(1)} collective-permute-done((f32[3,16,512]{2,1,0:T(8,128)S(1)}, f32[3,16,512]{2,1,0:T(8,128)S(1)}, u32[]{:S(2)}, u32[]{:S(2)}) %collective-permute-start.21) | collective-permute-done | bytes 98336 | tf_op jit(solution)/shard_map/ppermute | solution.py:290
  119.9 2.3 %collective-permute-start.23 = (f32[3,16,512]{2,1,0:T(8,128)S(1)}, f32[3,16,512]{2,1,0:T(8,128)S(1)}, u32[]{:S(2)}, u32[]{:S(2)}) collective-permute-start(f32[3,16,512]{2,1,0:T(8,128)S(1)} %add_add_fusion.6), channel_id=1, source_target_pairs={{0,16},{8,24},{16,0},{24,8},{32,48},{40,56},{48,32},{56,40},{64,80... | collective-permute-start | bytes 294920 | tf_op jit(solution)/shard_map/ppermute | solution.py:290
  122.2 2.7 %collective-permute-start.25 = (f32[3,16,512]{2,1,0:T(8,128)S(1)}, f32[3,16,512]{2,1,0:T(8,128)S(1)}, u32[]{:S(2)}, u32[]{:S(2)}) collective-permute-start(f32[3,16,512]{2,1,0:T(8,128)S(1)} %add_add_fusion.6), channel_id=1, source_target_pairs={{0,24},{8,0},{16,8},{24,16},{32,56},{40,32},{48,40},{56,48},{64,88... | collective-permute-start | bytes 294920 | tf_op jit(solution)/shard_map/ppermute | solution.py:290
  124.9 1.9 fusion.2
  126.8 3.1 %collective-permute-start.10 = (f32[2,128,512]{2,1,0:T(8,128)S(1)}, f32[2,128,512]{2,1,0:T(8,128)S(1)}, u32[]{:S(2)}, u32[]{:S(2)}) collective-permute-start(f32[2,128,512]{2,1,0:T(8,128)S(1)} %get-tuple-element.33), channel_id=1, source_target_pairs={{0,8},{1,121},{2,10},{3,123},{4,12},{5,125},{6,14},{7,127},{8,16},... | collective-permute-start | bytes 1572872 | tf_op jit(solution)/shard_map/ppermute | solution.py:290
  129.9 2.5 %collective-permute-start.12 = (f32[2,128,512]{2,1,0:T(8,128)S(1)}, f32[2,128,512]{2,1,0:T(8,128)S(1)}, u32[]{:S(2)}, u32[]{:S(2)}) collective-permute-start(f32[2,128,512]{2,1,0:T(8,128)S(1)} %get-tuple-element.32), channel_id=1, source_target_pairs={{0,8},{1,121},{2,10},{3,123},{4,12},{5,125},{6,14},{7,127},{8,16},... | collective-permute-start | bytes 1572872 | tf_op jit(solution)/shard_map/ppermute | solution.py:290
  132.4 3.4 %collective-permute-start.14 = (f32[2,128,512]{2,1,0:T(8,128)S(1)}, f32[2,128,512]{2,1,0:T(8,128)S(1)}, u32[]{:S(2)}, u32[]{:S(2)}) collective-permute-start(f32[2,128,512]{2,1,0:T(8,128)S(1)} %get-tuple-element.31), channel_id=1, source_target_pairs={{0,8},{1,121},{2,10},{3,123},{4,12},{5,125},{6,14},{7,127},{8,16},... | collective-permute-start | bytes 1572872 | tf_op jit(solution)/shard_map/ppermute | solution.py:290
  135.8 3.4 %collective-permute-start.8 = (f32[2,128,512]{2,1,0:T(8,128)S(1)}, f32[2,128,512]{2,1,0:T(8,128)S(1)}, u32[]{:S(2)}, u32[]{:S(2)}) collective-permute-start(f32[2,128,512]{2,1,0:T(8,128)S(1)} %get-tuple-element.30), channel_id=1, source_target_pairs={{0,8},{1,121},{2,10},{3,123},{4,12},{5,125},{6,14},{7,127},{8,16},... | collective-permute-start | bytes 1572872 | tf_op jit(solution)/shard_map/ppermute | solution.py:290
  139.3 0.9 constant_dynamic-update-slice_fusion.7
  140.2 0.4 collective-permute-start.26
  140.6 1.2 iota_compare_fusion
  141.8 20.6 %collective-permute-done.26 = f32[2,16,512]{2,1,0:T(8,128)S(1)} collective-permute-done((f32[2,16,512]{2,1,0:T(8,128)S(1)}, f32[2,16,512]{2,1,0:T(8,128)S(1)}, u32[]{:S(2)}, u32[]{:S(2)}) %collective-permute-start.26) | collective-permute-done | bytes 65568 | tf_op jit(solution)/shard_map/ppermute | solution.py:290
  162.5 4.3 %collective-permute-done.27 = f32[2,16,512]{2,1,0:T(8,128)S(1)} collective-permute-done((f32[2,16,512]{2,1,0:T(8,128)S(1)}, f32[2,16,512]{2,1,0:T(8,128)S(1)}, u32[]{:S(2)}, u32[]{:S(2)}) %collective-permute-start.27) | collective-permute-done | bytes 65568 | tf_op jit(solution)/shard_map/ppermute | solution.py:290
  166.8 3.1 %collective-permute-done.28 = f32[2,16,512]{2,1,0:T(8,128)S(1)} collective-permute-done((f32[2,16,512]{2,1,0:T(8,128)S(1)}, f32[2,16,512]{2,1,0:T(8,128)S(1)}, u32[]{:S(2)}, u32[]{:S(2)}) %collective-permute-start.28) | collective-permute-done | bytes 65568 | tf_op jit(solution)/shard_map/ppermute | solution.py:290
  169.9 0.7 collective-permute-start.29
  170.6 2.3 %collective-permute-start.30 = (f32[2,64,512]{2,1,0:T(8,128)S(1)}, f32[2,64,512]{2,1,0:T(8,128)S(1)}, u32[]{:S(2)}, u32[]{:S(2)}) collective-permute-start(f32[2,64,512]{2,1,0:T(8,128)S(1)} %constant_dynamic-update-slice_fusion.4), channel_id=1, source_target_pairs={{0,2},{1,3},{2,4},{3,5},{4,6},{5,7},{6,0},{7,1},{8,10},{9,11},{10,... | collective-permute-start | bytes 786440 | tf_op jit(solution)/shard_map/ppermute | solution.py:290
  173.0 1.9 select_add_fusion.3
  174.9 5.2 %collective-permute-start.11 = (f32[2,128,512]{2,1,0:T(8,128)}, f32[2,128,512]{2,1,0:T(8,128)}, u32[]{:S(2)}, u32[]{:S(2)}) collective-permute-start(f32[2,128,512]{2,1,0:T(8,128)} %get-tuple-element.21), channel_id=1, source_target_pairs={{0,1},{1,2},{2,3},{3,4},{4,5},{5,6},{6,7},{8,9},{9,10},{10,11},{11... | collective-permute-start | bytes 1572872 | tf_op jit(solution)/shard_map/ppermute | solution.py:290
  180.0 1.9 collective-permute-start.13
  182.2 4.8 %collective-permute-start.15 = (f32[2,128,512]{2,1,0:T(8,128)}, f32[2,128,512]{2,1,0:T(8,128)}, u32[]{:S(2)}, u32[]{:S(2)}) collective-permute-start(f32[2,128,512]{2,1,0:T(8,128)} %get-tuple-element.23), channel_id=1, source_target_pairs={{0,1},{1,2},{2,3},{3,4},{4,5},{5,6},{6,7},{8,9},{9,10},{10,11},{11... | collective-permute-start | bytes 1572872 | tf_op jit(solution)/shard_map/ppermute | solution.py:290
  187.0 1.9 collective-permute-start.9
  189.0 1.8 collective-permute-start.32
  190.9 0.6 iota_compare_fusion.3
  191.4 2.3 %collective-permute-done.13 = f32[2,128,512]{2,1,0:T(8,128)} collective-permute-done((f32[2,128,512]{2,1,0:T(8,128)}, f32[2,128,512]{2,1,0:T(8,128)}, u32[]{:S(2)}, u32[]{:S(2)}) %collective-permute-start.13) | collective-permute-done | bytes 524320 | tf_op jit(solution)/shard_map/ppermute | solution.py:290
  193.7 5.6 %collective-permute-done.15 = f32[2,128,512]{2,1,0:T(8,128)} collective-permute-done((f32[2,128,512]{2,1,0:T(8,128)}, f32[2,128,512]{2,1,0:T(8,128)}, u32[]{:S(2)}, u32[]{:S(2)}) %collective-permute-start.15) | collective-permute-done | bytes 524320 | tf_op jit(solution)/shard_map/ppermute | solution.py:290
  199.3 5.6 %collective-permute-done.9 = f32[2,128,512]{2,1,0:T(8,128)} collective-permute-done((f32[2,128,512]{2,1,0:T(8,128)}, f32[2,128,512]{2,1,0:T(8,128)}, u32[]{:S(2)}, u32[]{:S(2)}) %collective-permute-start.9) | collective-permute-done | bytes 524320 | tf_op jit(solution)/shard_map/ppermute | solution.py:290
  204.9 3.8 %add_add_fusion.3 = (f32[2,128,512]{2,1,0:T(8,128)S(1)}, f32[2,128,512]{2,1,0:T(8,128)S(1)}, f32[2,128,512]{2,1,0:T(8,128)S(1)}, f32[2,128,512]{2,1,0:T(8,128)S(1)}) fusion(f32[2,128,512]{2,1,0:T(8,128)} %collective-permute-done.9, f32[2,128,512]{2,1,0:T(8,128)} %copy-done.6, f32[2,512,512]{2,1,0:T(8,128)} %get-tuple-element.10, ...), kind=kLoop, calls=%fused_computation.8 | loop fusion | flops 2621440 | bytes 10486784 | tf_op jit(solution)/shard_map/add | solution.py:387
  208.8 1.5 pad_maximum_fusion
  210.3 1.4 broadcast_select_fusion.1
  211.7 1.5 pad_maximum_fusion.1
  (63 shorter events, 0.6 us)
Async XLA Ops:
  3.5 24.5 %collective-permute-start = (f32[2,128,512]{2,1,0:T(8,128)}, f32[2,128,512]{2,1,0:T(8,128)}, u32[]{:S(2)}, u32[]{:S(2)}) collective-permute-start(f32[2,128,512]{2,1,0:T(8,128)} %get-tuple-element.37), channel_id=1, source_target_pairs={{1,0},{2,1},{3,2},{4,3},{5,4},{6,5},{7,6},{9,8},{10,9},{11,10},{12... | collective-permute-start | bytes 1572872 | tf_op jit(solution)/shard_map/ppermute | solution.py:290
  6.8 21.2 %collective-permute-start.1 = (f32[2,128,512]{2,1,0:T(8,128)}, f32[2,128,512]{2,1,0:T(8,128)}, u32[]{:S(2)}, u32[]{:S(2)}) collective-permute-start(f32[2,128,512]{2,1,0:T(8,128)} %get-tuple-element.36), channel_id=1, source_target_pairs={{1,0},{2,1},{3,2},{4,3},{5,4},{6,5},{7,6},{9,8},{10,9},{11,10},{12... | collective-permute-start | bytes 1572872 | tf_op jit(solution)/shard_map/ppermute | solution.py:290
  8.8 19.3 %collective-permute-start.2 = (f32[2,128,512]{2,1,0:T(8,128)}, f32[2,128,512]{2,1,0:T(8,128)}, u32[]{:S(2)}, u32[]{:S(2)}) collective-permute-start(f32[2,128,512]{2,1,0:T(8,128)} %get-tuple-element.35), channel_id=1, source_target_pairs={{1,0},{2,1},{3,2},{4,3},{5,4},{6,5},{7,6},{9,8},{10,9},{11,10},{12... | collective-permute-start | bytes 1572872 | tf_op jit(solution)/shard_map/ppermute | solution.py:290
  10.7 22.0 %collective-permute-start.3 = (f32[2,128,512]{2,1,0:T(8,128)}, f32[2,128,512]{2,1,0:T(8,128)}, u32[]{:S(2)}, u32[]{:S(2)}) collective-permute-start(f32[2,128,512]{2,1,0:T(8,128)} %get-tuple-element.34), channel_id=1, source_target_pairs={{1,0},{2,1},{3,2},{4,3},{5,4},{6,5},{7,6},{9,8},{10,9},{11,10},{12... | collective-permute-start | bytes 1572872 | tf_op jit(solution)/shard_map/ppermute | solution.py:290
  19.7 7.0 %copy-start.8 = (s32[16,2]{0,1:T(2,128)S(1)}, s32[16,2]{0,1:T(2,128)}, u32[]{:S(2)}) copy-start(s32[16,2]{0,1:T(2,128)} %param.12) | copy-start | bytes 388
  19.7 12.9 %copy-start = (f32[2,512,512]{2,1,0:T(8,128)S(1)}, f32[2,512,512]{2,1,0:T(8,128)}, u32[]{:S(2)}) copy-start(f32[2,512,512]{2,1,0:T(8,128)} %tile.1) | copy-start | bytes 6291460
  19.7 36.0 %all-to-all-start = ((f32[16,32,512]{2,1,0:T(8,128)}), f32[16,32,512]{2,1,0:T(8,128)S(1)}, u32[]{:S(2)}, u32[]{:S(2)}) async-start(f32[16,32,512]{2,1,0:T(8,128)} %bin_frames.1), calls=%async_computation | async-start | bytes 2097152 | tf_op jit(solution)/shard_map/all_to_all | solution.py:369
  35.8 20.0 %collective-permute-start.4 = (f32[2,128,512]{2,1,0:T(8,128)}, f32[2,128,512]{2,1,0:T(8,128)S(1)}, u32[]{:S(2)}, u32[]{:S(2)}) collective-permute-start(f32[2,128,512]{2,1,0:T(8,128)} %get-tuple-element.27), channel_id=1, source_target_pairs={{1,9},{3,11},{5,13},{7,15},{8,0},{9,17},{10,2},{11,19},{12,4},{13,... | collective-permute-start | bytes 1572872 | tf_op jit(solution)/shard_map/ppermute | solution.py:290
  38.7 17.1 %collective-permute-start.5 = (f32[2,128,512]{2,1,0:T(8,128)}, f32[2,128,512]{2,1,0:T(8,128)S(1)}, u32[]{:S(2)}, u32[]{:S(2)}) collective-permute-start(f32[2,128,512]{2,1,0:T(8,128)} %get-tuple-element.25), channel_id=1, source_target_pairs={{1,9},{3,11},{5,13},{7,15},{8,0},{9,17},{10,2},{11,19},{12,4},{13,... | collective-permute-start | bytes 1572872 | tf_op jit(solution)/shard_map/ppermute | solution.py:290
  42.0 18.6 %collective-permute-start.6 = (f32[2,128,512]{2,1,0:T(8,128)}, f32[2,128,512]{2,1,0:T(8,128)S(1)}, u32[]{:S(2)}, u32[]{:S(2)}) collective-permute-start(f32[2,128,512]{2,1,0:T(8,128)} %get-tuple-element.26), channel_id=1, source_target_pairs={{1,9},{3,11},{5,13},{7,15},{8,0},{9,17},{10,2},{11,19},{12,4},{13,... | collective-permute-start | bytes 1572872 | tf_op jit(solution)/shard_map/ppermute | solution.py:290
  44.8 21.4 %collective-permute-start.7 = (f32[2,128,512]{2,1,0:T(8,128)}, f32[2,128,512]{2,1,0:T(8,128)S(1)}, u32[]{:S(2)}, u32[]{:S(2)}) collective-permute-start(f32[2,128,512]{2,1,0:T(8,128)} %get-tuple-element.24), channel_id=1, source_target_pairs={{1,9},{3,11},{5,13},{7,15},{8,0},{9,17},{10,2},{11,19},{12,4},{13,... | collective-permute-start | bytes 1572872 | tf_op jit(solution)/shard_map/ppermute | solution.py:290
  55.7 10.5 %copy-start.7 = (f32[16,32,512]{2,1,0:T(8,128)}, f32[16,32,512]{2,1,0:T(8,128)S(1)}, u32[]{:S(2)}) copy-start(f32[16,32,512]{2,1,0:T(8,128)S(1)} %all-to-all-done.binned) | copy-start | bytes 3145732
  55.7 10.5 %copy-start.9 = (f32[2,128,512]{2,1,0:T(8,128)}, f32[2,128,512]{2,1,0:T(8,128)S(1)}, u32[]{:S(2)}) copy-start(f32[2,128,512]{2,1,0:T(8,128)S(1)} %collective-permute-done.4.n0) | copy-start | bytes 1572868
  55.8 10.4 %copy-start.10 = (f32[2,128,512]{2,1,0:T(8,128)}, f32[2,128,512]{2,1,0:T(8,128)S(1)}, u32[]{:S(2)}) copy-start(f32[2,128,512]{2,1,0:T(8,128)S(1)} %collective-permute-done.5.n1) | copy-start | bytes 1572868
  60.6 5.6 %copy-start.11 = (f32[2,128,512]{2,1,0:T(8,128)}, f32[2,128,512]{2,1,0:T(8,128)S(1)}, u32[]{:S(2)}) copy-start(f32[2,128,512]{2,1,0:T(8,128)S(1)} %collective-permute-done.6.n2) | copy-start | bytes 1572868
  66.2 0.8 copy-start.12
  81.2 3.6 %collective-permute-start.16 = (f32[3,256,512]{2,1,0:T(8,128)}, f32[3,256,512]{2,1,0:T(8,128)S(1)}, u32[]{:S(2)}, u32[]{:S(2)}) collective-permute-start(f32[3,256,512]{2,1,0:T(8,128)} %get-tuple-element.13), channel_id=1, source_target_pairs={{0,1},{1,0},{2,3},{3,2},{4,5},{5,4},{6,7},{7,6},{8,9},{9,8},{10,11... | collective-permute-start | bytes 4718600 | tf_op jit(solution)/shard_map/ppermute | solution.py:290
  86.6 13.5 %collective-permute-start.17 = (f32[3,64,512]{2,1,0:T(8,128)S(1)}, f32[3,64,512]{2,1,0:T(8,128)S(1)}, u32[]{:S(2)}, u32[]{:S(2)}) collective-permute-start(f32[3,64,512]{2,1,0:T(8,128)S(1)} %get-tuple-element.38), channel_id=1, source_target_pairs={{0,4},{1,5},{2,6},{3,7},{4,0},{5,1},{6,2},{7,3},{8,12},{9,13},{10,... | collective-permute-start | bytes 1179656 | tf_op jit(solution)/shard_map/ppermute | solution.py:290
  90.7 18.0 %collective-permute-start.18 = (f32[3,64,512]{2,1,0:T(8,128)S(1)}, f32[3,64,512]{2,1,0:T(8,128)S(1)}, u32[]{:S(2)}, u32[]{:S(2)}) collective-permute-start(f32[3,64,512]{2,1,0:T(8,128)S(1)} %get-tuple-element.40), channel_id=1, source_target_pairs={{0,2},{1,3},{2,4},{3,5},{4,6},{5,7},{6,0},{7,1},{8,10},{9,11},{10,... | collective-permute-start | bytes 1179656 | tf_op jit(solution)/shard_map/ppermute | solution.py:290
  93.1 17.7 %collective-permute-start.19 = (f32[3,64,512]{2,1,0:T(8,128)S(1)}, f32[3,64,512]{2,1,0:T(8,128)}, u32[]{:S(2)}, u32[]{:S(2)}) collective-permute-start(f32[3,64,512]{2,1,0:T(8,128)S(1)} %get-tuple-element.39), channel_id=1, source_target_pairs={{0,6},{1,7},{2,0},{3,1},{4,2},{5,3},{6,4},{7,5},{8,14},{9,15},{10,... | collective-permute-start | bytes 1179656 | tf_op jit(solution)/shard_map/ppermute | solution.py:290
  111.9 5.4 %collective-permute-start.20 = (f32[3,16,512]{2,1,0:T(8,128)S(1)}, f32[3,16,512]{2,1,0:T(8,128)S(1)}, u32[]{:S(2)}, u32[]{:S(2)}) collective-permute-start(f32[3,16,512]{2,1,0:T(8,128)S(1)} %get-tuple-element.41), channel_id=1, source_target_pairs={{0,64},{8,72},{16,80},{24,88},{32,96},{40,104},{48,112},{56,120},{... | collective-permute-start | bytes 294920 | tf_op jit(solution)/shard_map/ppermute | solution.py:290
  112.8 7.1 %collective-permute-start.21 = (f32[3,16,512]{2,1,0:T(8,128)S(1)}, f32[3,16,512]{2,1,0:T(8,128)S(1)}, u32[]{:S(2)}, u32[]{:S(2)}) collective-permute-start(f32[3,16,512]{2,1,0:T(8,128)S(1)} %get-tuple-element.43), channel_id=1, source_target_pairs={{0,32},{8,40},{16,48},{24,56},{32,64},{40,72},{48,80},{56,88},{64,... | collective-permute-start | bytes 294920 | tf_op jit(solution)/shard_map/ppermute | solution.py:290
  113.0 6.9 %collective-permute-start.22 = (f32[3,16,512]{2,1,0:T(8,128)S(1)}, f32[3,16,512]{2,1,0:T(8,128)S(1)}, u32[]{:S(2)}, u32[]{:S(2)}) collective-permute-start(f32[3,16,512]{2,1,0:T(8,128)S(1)} %get-tuple-element.42), channel_id=1, source_target_pairs={{0,96},{8,104},{16,112},{24,120},{32,0},{40,8},{48,16},{56,24},{64... | collective-permute-start | bytes 294920 | tf_op jit(solution)/shard_map/ppermute | solution.py:290
  119.9 12.5 %collective-permute-start.23 = (f32[3,16,512]{2,1,0:T(8,128)S(1)}, f32[3,16,512]{2,1,0:T(8,128)S(1)}, u32[]{:S(2)}, u32[]{:S(2)}) collective-permute-start(f32[3,16,512]{2,1,0:T(8,128)S(1)} %add_add_fusion.6), channel_id=1, source_target_pairs={{0,16},{8,24},{16,0},{24,8},{32,48},{40,56},{48,32},{56,40},{64,80... | collective-permute-start | bytes 294920 | tf_op jit(solution)/shard_map/ppermute | solution.py:290
  122.2 13.6 %collective-permute-start.24 = (f32[3,16,512]{2,1,0:T(8,128)S(1)}, f32[3,16,512]{2,1,0:T(8,128)S(1)}, u32[]{:S(2)}, u32[]{:S(2)}) collective-permute-start(f32[3,16,512]{2,1,0:T(8,128)S(1)} %add_add_fusion.6), channel_id=1, source_target_pairs={{0,8},{8,16},{16,24},{24,0},{32,40},{40,48},{48,56},{56,32},{64,72... | collective-permute-start | bytes 294920 | tf_op jit(solution)/shard_map/ppermute | solution.py:290
  122.2 17.0 %collective-permute-start.25 = (f32[3,16,512]{2,1,0:T(8,128)S(1)}, f32[3,16,512]{2,1,0:T(8,128)S(1)}, u32[]{:S(2)}, u32[]{:S(2)}) collective-permute-start(f32[3,16,512]{2,1,0:T(8,128)S(1)} %add_add_fusion.6), channel_id=1, source_target_pairs={{0,24},{8,0},{16,8},{24,16},{32,56},{40,32},{48,40},{56,48},{64,88... | collective-permute-start | bytes 294920 | tf_op jit(solution)/shard_map/ppermute | solution.py:290
  124.9 48.1 %copy-start.2 = (f32[2,512,512]{2,1,0:T(8,128)S(1)}, f32[2,512,512]{2,1,0:T(8,128)}, u32[]{:S(2)}) copy-start(f32[2,512,512]{2,1,0:T(8,128)} %get-tuple-element.10) | copy-start | bytes 6291460
  126.8 43.8 %collective-permute-start.10 = (f32[2,128,512]{2,1,0:T(8,128)S(1)}, f32[2,128,512]{2,1,0:T(8,128)S(1)}, u32[]{:S(2)}, u32[]{:S(2)}) collective-permute-start(f32[2,128,512]{2,1,0:T(8,128)S(1)} %get-tuple-element.33), channel_id=1, source_target_pairs={{0,8},{1,121},{2,10},{3,123},{4,12},{5,125},{6,14},{7,127},{8,16},... | collective-permute-start | bytes 1572872 | tf_op jit(solution)/shard_map/ppermute | solution.py:290
  129.9 43.0 %collective-permute-start.12 = (f32[2,128,512]{2,1,0:T(8,128)S(1)}, f32[2,128,512]{2,1,0:T(8,128)S(1)}, u32[]{:S(2)}, u32[]{:S(2)}) collective-permute-start(f32[2,128,512]{2,1,0:T(8,128)S(1)} %get-tuple-element.32), channel_id=1, source_target_pairs={{0,8},{1,121},{2,10},{3,123},{4,12},{5,125},{6,14},{7,127},{8,16},... | collective-permute-start | bytes 1572872 | tf_op jit(solution)/shard_map/ppermute | solution.py:290
  132.4 40.5 %collective-permute-start.14 = (f32[2,128,512]{2,1,0:T(8,128)S(1)}, f32[2,128,512]{2,1,0:T(8,128)S(1)}, u32[]{:S(2)}, u32[]{:S(2)}) collective-permute-start(f32[2,128,512]{2,1,0:T(8,128)S(1)} %get-tuple-element.31), channel_id=1, source_target_pairs={{0,8},{1,121},{2,10},{3,123},{4,12},{5,125},{6,14},{7,127},{8,16},... | collective-permute-start | bytes 1572872 | tf_op jit(solution)/shard_map/ppermute | solution.py:290
  135.8 37.1 %collective-permute-start.8 = (f32[2,128,512]{2,1,0:T(8,128)S(1)}, f32[2,128,512]{2,1,0:T(8,128)S(1)}, u32[]{:S(2)}, u32[]{:S(2)}) collective-permute-start(f32[2,128,512]{2,1,0:T(8,128)S(1)} %get-tuple-element.30), channel_id=1, source_target_pairs={{0,8},{1,121},{2,10},{3,123},{4,12},{5,125},{6,14},{7,127},{8,16},... | collective-permute-start | bytes 1572872 | tf_op jit(solution)/shard_map/ppermute | solution.py:290
  140.2 22.3 %collective-permute-start.26 = (f32[2,16,512]{2,1,0:T(8,128)S(1)}, f32[2,16,512]{2,1,0:T(8,128)S(1)}, u32[]{:S(2)}, u32[]{:S(2)}) collective-permute-start(f32[2,16,512]{2,1,0:T(8,128)S(1)} %get-tuple-element.15), channel_id=1, source_target_pairs={{0,64},{8,72},{16,80},{24,88},{32,96},{40,104},{48,112},{56,120},{... | collective-permute-start | bytes 196616 | tf_op jit(solution)/shard_map/ppermute | solution.py:290
  162.5 4.3 %collective-permute-start.27 = (f32[2,16,512]{2,1,0:T(8,128)S(1)}, f32[2,16,512]{2,1,0:T(8,128)S(1)}, u32[]{:S(2)}, u32[]{:S(2)}) collective-permute-start(f32[2,16,512]{2,1,0:T(8,128)S(1)} %get-tuple-element.15), channel_id=1, source_target_pairs={{0,32},{8,40},{16,48},{24,56},{32,64},{40,72},{48,80},{56,88},{64,... | collective-permute-start | bytes 196616 | tf_op jit(solution)/shard_map/ppermute | solution.py:290
  166.8 3.1 %collective-permute-start.28 = (f32[2,16,512]{2,1,0:T(8,128)S(1)}, f32[2,16,512]{2,1,0:T(8,128)S(1)}, u32[]{:S(2)}, u32[]{:S(2)}) collective-permute-start(f32[2,16,512]{2,1,0:T(8,128)S(1)} %get-tuple-element.15), channel_id=1, source_target_pairs={{0,96},{8,104},{16,112},{24,120},{32,0},{40,8},{48,16},{56,24},{64... | collective-permute-start | bytes 196616 | tf_op jit(solution)/shard_map/ppermute | solution.py:290
  169.9 12.3 %collective-permute-start.29 = (f32[2,64,512]{2,1,0:T(8,128)S(1)}, f32[2,64,512]{2,1,0:T(8,128)S(1)}, u32[]{:S(2)}, u32[]{:S(2)}) collective-permute-start(f32[2,64,512]{2,1,0:T(8,128)S(1)} %constant_dynamic-update-slice_fusion.4), channel_id=1, source_target_pairs={{0,4},{1,5},{2,6},{3,7},{4,0},{5,1},{6,2},{7,3},{8,12},{9,13},{10,... | collective-permute-start | bytes 786440 | tf_op jit(solution)/shard_map/ppermute | solution.py:290
  170.6 4.2 %copy-start.3 = (f32[2,128,512]{2,1,0:T(8,128)}, f32[2,128,512]{2,1,0:T(8,128)S(1)}, u32[]{:S(2)}) copy-start(f32[2,128,512]{2,1,0:T(8,128)S(1)} %collective-permute-done.10) | copy-start | bytes 1572868
  170.6 16.4 %collective-permute-start.30 = (f32[2,64,512]{2,1,0:T(8,128)S(1)}, f32[2,64,512]{2,1,0:T(8,128)S(1)}, u32[]{:S(2)}, u32[]{:S(2)}) collective-permute-start(f32[2,64,512]{2,1,0:T(8,128)S(1)} %constant_dynamic-update-slice_fusion.4), channel_id=1, source_target_pairs={{0,2},{1,3},{2,4},{3,5},{4,6},{5,7},{6,0},{7,1},{8,10},{9,11},{10,... | collective-permute-start | bytes 786440 | tf_op jit(solution)/shard_map/ppermute | solution.py:290
  172.9 1.9 copy-start.4
  172.9 1.9 copy-start.5
  173.0 1.9 copy-start.6
  174.8 30.1 %copy-start.1 = (f32[2,512,512]{2,1,0:T(8,128)S(1)}, f32[2,512,512]{2,1,0:T(8,128)}, u32[]{:S(2)}) copy-start(f32[2,512,512]{2,1,0:T(8,128)} %tile.1) | copy-start | bytes 6291460
  174.9 16.6 %collective-permute-start.11 = (f32[2,128,512]{2,1,0:T(8,128)}, f32[2,128,512]{2,1,0:T(8,128)}, u32[]{:S(2)}, u32[]{:S(2)}) collective-permute-start(f32[2,128,512]{2,1,0:T(8,128)} %get-tuple-element.21), channel_id=1, source_target_pairs={{0,1},{1,2},{2,3},{3,4},{4,5},{5,6},{6,7},{8,9},{9,10},{10,11},{11... | collective-permute-start | bytes 1572872 | tf_op jit(solution)/shard_map/ppermute | solution.py:290
  180.0 13.7 %collective-permute-start.13 = (f32[2,128,512]{2,1,0:T(8,128)}, f32[2,128,512]{2,1,0:T(8,128)}, u32[]{:S(2)}, u32[]{:S(2)}) collective-permute-start(f32[2,128,512]{2,1,0:T(8,128)} %get-tuple-element.22), channel_id=1, source_target_pairs={{0,1},{1,2},{2,3},{3,4},{4,5},{5,6},{6,7},{8,9},{9,10},{10,11},{11... | collective-permute-start | bytes 1572872 | tf_op jit(solution)/shard_map/ppermute | solution.py:290
  182.0 7.0 %collective-permute-start.31 = (f32[2,64,512]{2,1,0:T(8,128)S(1)}, f32[2,64,512]{2,1,0:T(8,128)S(1)}, u32[]{:S(2)}, u32[]{:S(2)}) collective-permute-start(f32[2,64,512]{2,1,0:T(8,128)S(1)} %constant_dynamic-update-slice_fusion.4), channel_id=1, source_target_pairs={{0,6},{1,7},{2,0},{3,1},{4,2},{5,3},{6,4},{7,5},{8,14},{9,15},{10,... | collective-permute-start | bytes 786440 | tf_op jit(solution)/shard_map/ppermute | solution.py:290
  182.2 17.1 %collective-permute-start.15 = (f32[2,128,512]{2,1,0:T(8,128)}, f32[2,128,512]{2,1,0:T(8,128)}, u32[]{:S(2)}, u32[]{:S(2)}) collective-permute-start(f32[2,128,512]{2,1,0:T(8,128)} %get-tuple-element.23), channel_id=1, source_target_pairs={{0,1},{1,2},{2,3},{3,4},{4,5},{5,6},{6,7},{8,9},{9,10},{10,11},{11... | collective-permute-start | bytes 1572872 | tf_op jit(solution)/shard_map/ppermute | solution.py:290
  187.0 17.9 %collective-permute-start.9 = (f32[2,128,512]{2,1,0:T(8,128)}, f32[2,128,512]{2,1,0:T(8,128)}, u32[]{:S(2)}, u32[]{:S(2)}) collective-permute-start(f32[2,128,512]{2,1,0:T(8,128)} %get-tuple-element.20), channel_id=1, source_target_pairs={{0,1},{1,2},{2,3},{3,4},{4,5},{5,6},{6,7},{8,9},{9,10},{10,11},{11... | collective-permute-start | bytes 1572872 | tf_op jit(solution)/shard_map/ppermute | solution.py:290
  189.0 21.2 %collective-permute-start.32 = (f32[2,256,512]{2,1,0:T(8,128)S(1)}, f32[2,256,512]{2,1,0:T(8,128)}, u32[]{:S(2)}, u32[]{:S(2)}) collective-permute-start(f32[2,256,512]{2,1,0:T(8,128)S(1)} %constant_dynamic-update-slice_fusion), channel_id=1, source_target_pairs={{0,1},{1,0},{2,3},{3,2},{4,5},{5,4},{6,7},{7,6},{8,9},{9,8},{10,11... | collective-permute-start | bytes 3145736 | tf_op jit(solution)/shard_map/ppermute | solution.py:290

commit v2 on v1

v2 whole, which is shorter than its diff:
```python
import functools
import math

import jax
import jax.numpy as jnp
import ml_dtypes
import numpy as np
from jax import lax
from jax.experimental import pallas as pl
from jax.experimental.pallas import tpu as pltpu
from jax.sharding import PartitionSpec as P

SIDE = 512
QUARTER = 128
ROWS = 16
COLS = 8
STRIP = 16
CUT = 320
BOTH = ("readout", "pos")
F32 = jnp.float32
BF16 = jnp.bfloat16
VMEM_BYTES = 56 * 1024 * 1024


def split_table(table):
    high = table.astype(ml_dtypes.bfloat16)
    low = (table - high.astype(np.float64)).astype(ml_dtypes.bfloat16)
    return np.stack([high, low])


@functools.cache
def dft_tables():
    index = np.arange(QUARTER)
    tables = []
    for group in range(4):
        product_mod = (index[:, None] * (4 * index[None, :] + group)) % SIDE
        angles = product_mod * (2.0 * math.pi / SIDE)
        cosine = np.cos(angles) / math.sqrt(SIDE)
        sine = np.sin(angles) / math.sqrt(SIDE)
        tables.append(np.block([[cosine, -sine], [sine, cosine]]))
    straight = np.stack([split_table(table) for table in tables])
    turned = np.stack([split_table(table.T) for table in tables])
    return straight, turned


@functools.cache
def pair_table():
    table = np.zeros((2 * SIDE, SIDE), np.float32)
    for group in range(4):
        for place in range(QUARTER):
            for u in range(2):
                table[8 * place + 2 * group + u, group * QUARTER + place] = 1.0
    return table.astype(ml_dtypes.bfloat16)


def my_place():
    r = lax.axis_index("readout")
    p = lax.axis_index("pos")
    return r, lax.rem(r, 4), r // 4, p // 2, lax.rem(p, 2)


def split_two(values):
    high = values.astype(BF16)
    low = (values - high.astype(F32)).astype(BF16)
    return high, low


def bin_kernel(frames, dark, gain, pairs, out, lanes, sums):
    step = pl.program_id(0)
    flip = my_place()[4]
    count = frames.shape[0]
    for n in range(count):
        corrected = jnp.maximum(frames[n] - dark[...], 0.0) * gain[...]
        for t in range(8):
            lanes[8 * n + t] = corrected[:, QUARTER * t : QUARTER * (t + 1)]
        for t in range(8):
            for group in range(4):
                total = lanes[8 * n + t, pl.ds(2 * group, 8, stride=8), :]
                total += lanes[8 * n + t, pl.ds(2 * group + 1, 8, stride=8), :]
                first = 32 * n + 8 * group
                sums[first : first + 8, QUARTER * t : QUARTER * (t + 1)] = total
    values = sums[...]
    high = values.astype(BF16)
    rest = values - high.astype(F32)
    mid = rest.astype(BF16)
    low = (rest - mid.astype(F32)).astype(BF16)
    table = pairs[...]
    binned = jnp.dot(low, table, preferred_element_type=F32)
    binned += jnp.dot(mid, table, preferred_element_type=F32)
    binned += jnp.dot(high, table, preferred_element_type=F32)
    for n in range(count):
        place = lax.rem(step * count + n + flip, ROWS)
        out[place] = binned[32 * n : 32 * n + 32, :]


def bin_frames(frames, dark, gain):
    per_step = 8
    return pl.pallas_call(
        bin_kernel,
        out_shape=jax.ShapeDtypeStruct((ROWS, 32, SIDE), F32),
        grid=(ROWS // per_step,),
        in_specs=[
            pl.BlockSpec((per_step, 64, 2 * SIDE), lambda s: (s, 0, 0)),
            pl.BlockSpec((64, 2 * SIDE), lambda s: (0, 0)),
            pl.BlockSpec((64, 2 * SIDE), lambda s: (0, 0)),
            pl.BlockSpec((2 * SIDE, SIDE), lambda s: (0, 0)),
        ],
        out_specs=pl.BlockSpec((ROWS, 32, SIDE), lambda s: (0, 0, 0)),
        scratch_shapes=[
            pltpu.VMEM((8 * per_step, 64, QUARTER), F32),
            pltpu.VMEM((32 * per_step, 2 * SIDE), F32),
        ],
        compiler_params=pltpu.CompilerParams(vmem_limit_bytes=VMEM_BYTES),
        cost_estimate=pl.CostEstimate(flops=0, bytes_accessed=0, transcendentals=0),
        name="bin_frames",
    )(frames, dark, gain, jnp.asarray(pair_table()))


def roll_both(values, down, right):
    return pltpu.roll(pltpu.roll(values, down, 0), right, 1)


def roll_kernel(offsets, probe, out, peak):
    r, _, _, _, flip = my_place()
    position = lax.rem(r - flip + ROWS, ROWS)
    o0, o1 = offsets[position, 0], offsets[position, 1]
    real = probe[0]
    imag = probe[1]
    peak[...] = jnp.broadcast_to(jnp.max(real * real + imag * imag, keepdims=True), (8, 128))
    out[0] = roll_both(real, o0, o1)
    out[1] = roll_both(imag, o0, o1)


def roll_probe(offset, probe):
    return pl.pallas_call(
        roll_kernel,
        out_shape=[jax.ShapeDtypeStruct((2, SIDE, SIDE), F32), jax.ShapeDtypeStruct((8, 128), F32)],
        in_specs=[pl.BlockSpec(memory_space=pltpu.SMEM), pl.BlockSpec(memory_space=pltpu.VMEM)],
        out_specs=[pl.BlockSpec(memory_space=pltpu.VMEM)] * 2,
        compiler_params=pltpu.CompilerParams(vmem_limit_bytes=VMEM_BYTES),
        cost_estimate=pl.CostEstimate(flops=2**22, bytes_accessed=64 * 2**20, transcendentals=0),
        name="roll_probe",
    )(offset, probe)


def times_i(pair):
    return -pair[1], pair[0]


def add(one, two):
    return one[0] + two[0], one[1] + two[1]


def sub(one, two):
    return one[0] - two[0], one[1] - two[1]


def butterfly(x0, x1, x2, x3, sign):
    even_sum, even_diff = add(x0, x2), sub(x0, x2)
    odd_sum, odd_diff = add(x1, x3), sub(x1, x3)
    turned = times_i(odd_diff)
    if sign < 0:
        first, third = sub(even_diff, turned), add(even_diff, turned)
    else:
        first, third = add(even_diff, turned), sub(even_diff, turned)
    return add(even_sum, odd_sum), first, sub(even_sum, odd_sum), third


def three_dots(left_high, left_low, right_high, right_low):
    total = jnp.dot(left_high, right_high, preferred_element_type=F32)
    total += jnp.dot(left_high, right_low, preferred_element_type=F32)
    total += jnp.dot(left_low, right_high, preferred_element_type=F32)
    return total


def strip_rows(core, z, y):
    start = core * (SIDE // 2) + lax.rem(z, 4) * (SIDE // 8) + lax.rem(y, 4) * STRIP
    return pl.ds(pl.multiple_of(start, STRIP), STRIP)


def main_kernel(
    offsets, tile_hbm, r0_hbm, r1_hbm, n0_hbm, n1_hbm, probe_hbm, binned_hbm, straight_hbm, turned_hbm, peak,
    change, sum_away, sum_kept,
    patch, wave, wide, mid_high, mid_low, full, tile, right, other, probe, binned, straight, turned, sems,
):
    r, _, y, z, core = my_place()
    position = lax.rem(r - core + ROWS, ROWS)
    o0, o1 = offsets[position, 0], offsets[position, 1]
    own_from = jnp.where(core == 1, 0, o0)
    own_to = jnp.where(core == 1, o0, SIDE)
    valid = jnp.where((core == 1) & (r == 0), 0, 1)
    quarters = [slice(QUARTER * a, QUARTER * (a + 1)) for a in range(4)]
    halves = [slice(0, QUARTER), slice(QUARTER, 2 * QUARTER)]

    early, late = [], []

    def fetch(group, source, target):
        copy = pltpu.make_async_copy(source, target, sems.at[len(early) + len(late)])
        copy.start()
        group.append(copy)

    for source0, source1, target in ((r0_hbm, r1_hbm, right), (n0_hbm, n1_hbm, other)):
        fetch(early, source0, target.at[:, :CUT])
        fetch(early, source1, target.at[:, CUT:])
    for piece in (slice(0, SIDE // 2), slice(SIDE // 2, SIDE)):
        fetch(early, tile_hbm.at[:, piece], tile.at[:, piece])
        fetch(early, probe_hbm.at[:, piece], probe.at[:, piece])
    fetch(late, straight_hbm, straight)
    fetch(late, turned_hbm, turned)
    fetch(late, binned_hbm, binned)
    step = QUARTER // 2
    for n in range(8):
        if n == 0:
            for k in (0, 2, 4, 5):
                early[k].wait()
        if n == 4:
            for k in (1, 3, 6, 7):
                early[k].wait()
        piece = slice(step * n, step * (n + 1))
        rows = lax.broadcasted_iota(jnp.int32, (step, SIDE), 0) + step * n
        cols = lax.broadcasted_iota(jnp.int32, (step, SIDE), 1)
        own = (rows >= own_from) & (rows < own_to)
        here = cols >= o1
        obj = []
        for part in range(2):
            mine = jnp.where(here, tile[part, piece, :], right[part, piece, :])
            mine = jnp.where(valid == 1, mine, 0.0)
            obj.append(jnp.where(own, mine, other[part, piece, :]))
            patch[part, piece, :] = obj[part]
        pr = probe[0, piece, :], probe[1, piece, :]
        wave[0, piece, :] = pr[0] * obj[0] - pr[1] * obj[1]
        wave[1, piece, :] = pr[0] * obj[1] + pr[1] * obj[0]
    for a in range(4):
        blocks = [(wave[0, quarters[a], quarters[b]], wave[1, quarters[a], quarters[b]]) for b in range(4)]
        for g, pair in enumerate(butterfly(*blocks, -1)):
            for part in range(2):
                mid_high[g, quarters[a], halves[part]], mid_low[g, quarters[a], halves[part]] = split_two(pair[part])

    late[0].wait()
    for g in range(4):
        out = three_dots(mid_high[g], mid_low[g], straight[g, 0], straight[g, 1])
        wide[0, :, quarters[g]] = out[:, :QUARTER]
        wide[1, :, quarters[g]] = out[:, QUARTER:]

    for b in range(4):
        blocks = [(wide[0, quarters[a], quarters[b]], wide[1, quarters[a], quarters[b]]) for a in range(4)]
        for h, pair in enumerate(butterfly(*blocks, -1)):
            for part in range(2):
                high, low = split_two(pair[part])
                full[h, 0, halves[part], quarters[b]] = high
                full[h, 1, halves[part], quarters[b]] = low

    late[1].wait()
    late[2].wait()
    for h in range(4):
        spec = three_dots(turned[h, 0], turned[h, 1], full[h, 0], full[h, 1])
        real, imag = spec[:QUARTER], spec[QUARTER:]
        power = real * real + imag * imag
        level = binned[:, 8 * h : 8 * h + 8, :].reshape(QUARTER, SIDE)
        factor = jnp.sqrt(level) * lax.rsqrt(jnp.maximum(power, 0.0625))
        for part, value in enumerate((real * factor, imag * factor)):
            high, low = split_two(value)
            full[h, 0, halves[part], :] = high
            full[h, 1, halves[part], :] = low

    for h in range(4):
        back = three_dots(straight[h, 0], straight[h, 1], full[h, 0], full[h, 1])
        wide[0, quarters[h], :] = back[:QUARTER]
        wide[1, quarters[h], :] = back[QUARTER:]

    for b in range(4):
        blocks = [(wide[0, quarters[h], quarters[b]], wide[1, quarters[h], quarters[b]]) for h in range(4)]
        for a, pair in enumerate(butterfly(*blocks, 1)):
            for part in range(2):
                mid_high[b, quarters[a], halves[part]], mid_low[b, quarters[a], halves[part]] = split_two(pair[part])

    for g in range(4):
        out = three_dots(mid_high[g], mid_low[g], turned[g, 0], turned[g, 1])
        wide[0, :, quarters[g]] = out[:, :QUARTER]
        wide[1, :, quarters[g]] = out[:, QUARTER:]

    scale = 1.0 / peak[0:1, 0:1]
    for a in range(4):
        blocks = [(wide[0, quarters[a], quarters[g]], wide[1, quarters[a], quarters[g]]) for g in range(4)]
        for b, back in enumerate(butterfly(*blocks, 1)):
            at = (quarters[a], quarters[b])
            dr = back[0] - wave[0, at[0], at[1]]
            di = back[1] - wave[1, at[0], at[1]]
            pr, pi = probe[0, at[0], at[1]], probe[1, at[0], at[1]]
            change[0, at[0], at[1]] = (pr * dr + pi * di) * scale
            change[1, at[0], at[1]] = (pr * di - pi * dr) * scale
            cr, ci = patch[0, at[0], at[1]], patch[1, at[0], at[1]]
            wide[0, at[0], at[1]] = cr * dr + ci * di
            wide[1, at[0], at[1]] = cr * di - ci * dr
            wide[2, at[0], at[1]] = cr * cr + ci * ci

    up = lax.rem(SIDE - o0, SIDE)
    left = lax.rem(SIDE - o1, SIDE)
    for part in range(3):
        wide[part] = roll_both(wide[part], up, left)
        for i in range(4):
            for j in range(4):
                sum_kept[i, j, part] = wide[part, strip_rows(core, z + i, y + j), :]
                sum_away[i, j, part] = wide[part, strip_rows(1 - core, z + i, y + j), :]


def main_call(offsets, tile, rights, others, probe, binned, peak):
    straight, turned = dft_tables()
    whole = (2, SIDE, SIDE)
    half = (4, 4, 3, STRIP, SIDE)
    vmem = pl.BlockSpec(memory_space=pltpu.VMEM)
    anywhere = pl.BlockSpec(memory_space=pl.ANY)
    tables = (4, 2, 2 * QUARTER, 2 * QUARTER)
    return pl.pallas_call(
        main_kernel,
        out_shape=[jax.ShapeDtypeStruct(s, F32) for s in (whole, half, half)],
        in_specs=[pl.BlockSpec(memory_space=pltpu.SMEM)] + [anywhere] * 9 + [vmem],
        out_specs=[vmem] * 3,
        scratch_shapes=[
            pltpu.VMEM(whole, F32),
            pltpu.VMEM(whole, F32),
            pltpu.VMEM((3, SIDE, SIDE), F32),
            pltpu.VMEM((4, SIDE, 2 * QUARTER), BF16),
            pltpu.VMEM((4, SIDE, 2 * QUARTER), BF16),
            pltpu.VMEM((4, 2, 2 * QUARTER, SIDE), BF16),
            pltpu.VMEM(whole, F32),
            pltpu.VMEM(whole, F32),
            pltpu.VMEM(whole, F32),
            pltpu.VMEM(whole, F32),
            pltpu.VMEM((ROWS, 32, SIDE), F32),
            pltpu.VMEM(tables, BF16),
            pltpu.VMEM(tables, BF16),
            pltpu.SemaphoreType.DMA((11,)),
        ],
        compiler_params=pltpu.CompilerParams(vmem_limit_bytes=VMEM_BYTES),
        cost_estimate=pl.CostEstimate(flops=8 * 2**30, bytes_accessed=20 * 2**20, transcendentals=2**19),
        name="phase_update",
    )(offsets, tile, *rights, *others, probe, binned, jnp.asarray(straight), jnp.asarray(turned), peak)


def send(block, axis, route):
    return lax.ppermute(block, axis, route)


def device_pairs(move):
    pairs = []
    for r in range(ROWS):
        for p in range(COLS):
            target = move(r, p)
            if target is not None:
                pairs.append((r * COLS + p, target[0] * COLS + target[1]))
    return pairs


def gather_pairs(r, p):
    if p % 2 == 0:
        return (r - 1, p) if r > 0 else None
    return ((r + 1) % ROWS, p)


def scatter_pairs(r, p):
    if p % 2 == 0:
        return (r + 1, p) if r < ROWS - 1 else None
    return ((r - 1) % ROWS, p)


def ring_z(distance):
    return [(p, (p + 2 * distance) % COLS) for p in range(COLS)]


def ring_y(distance):
    return [(r, (r + 4 * distance) % ROWS) for r in range(ROWS)]


def ring_x(distance):
    return [(r, r // 4 * 4 + (r + distance) % 4) for r in range(ROWS)]


def around(values, axis, ring):
    return [send(values, axis, ring(k)) for k in (1, 2, 3)]


def scatter_sum(values, axis, ring):
    first, second, third = (send(values[k], axis, ring(k)) for k in (1, 2, 3))
    return (values[0] + second) + (first + third)


def place_kernel(o0, o1, o2, o3, other, out):
    _, _, y, z, core = my_place()
    for i, own in enumerate((o0, o1, o2, o3)):
        for j in range(4):
            for part in range(2):
                out[part, strip_rows(core, z + 4 - i, y + 4 - j), :] = own[j, part]
                out[part, strip_rows(1 - core, z + 4 - i, y + 4 - j), :] = other[i, j, part]


def place_strips(own, other):
    vmem = pl.BlockSpec(memory_space=pltpu.VMEM)
    return pl.pallas_call(
        place_kernel,
        out_shape=jax.ShapeDtypeStruct((2, SIDE, SIDE), F32),
        in_specs=[vmem] * 5,
        out_specs=vmem,
        compiler_params=pltpu.CompilerParams(vmem_limit_bytes=VMEM_BYTES),
        cost_estimate=pl.CostEstimate(flops=0, bytes_accessed=4 * 2**20, transcendentals=0),
        name="place_strips",
    )(*own, other)


def on_device(frames, dark, gain, offsets, object_field, probe):
    r = lax.axis_index("readout")
    p = lax.axis_index("pos")
    flip = lax.rem(p, 2)
    z = p // 2
    x, y = lax.rem(r, 4), r // 4
    position = lax.rem(r - flip + ROWS, ROWS)
    beside = lax.rem(r - 1 + flip + ROWS, ROWS)
    o1 = offsets[position, 1]
    o1_beside = offsets[beside, 1]

    to_left = [(i, i - 1) for i in range(1, COLS)]
    to_right = [(i, i + 1) for i in range(COLS - 1)]
    swap_cores = [(i, i ^ 1) for i in range(COLS)]
    half = SIDE // 2
    chunks = [object_field[:, :CUT], object_field[:, CUT:]]
    chunks = lax.optimization_barrier(chunks)
    rights = [send(chunk, "pos", to_left) for chunk in chunks]
    binned = bin_frames(frames, dark, gain)
    cols = lax.broadcasted_iota(jnp.int32, (2, SIDE, SIDE), 2)
    regrouped = lax.all_to_all(binned, "readout", split_axis=0, concat_axis=0, tiled=True)
    joined = []
    for a in range(2):
        before = (joined[0], regrouped) if a > 0 else binned
        rights[a], _ = lax.optimization_barrier((rights[a], before))
        joined.append(jnp.where(cols[:, : chunks[a].shape[1]] >= o1_beside, chunks[a], rights[a]))
    others = [send(block, BOTH, device_pairs(gather_pairs)) for block in joined]
    rolled, peak = roll_probe(offsets, probe)

    change, sum_away, sum_kept = main_call(offsets, object_field, rights, others, rolled, regrouped, peak)

    rows = lax.broadcasted_iota(jnp.int32, (2, SIDE, SIDE), 1)
    upper, upper_beside = rows >= offsets[position, 0], rows >= offsets[beside, 0]
    mine = ((flip == 0) & upper) | ((flip == 1) & (r > 0) & ~upper)
    theirs = ((flip == 0) & ~upper_beside) | ((flip == 1) & upper_beside)

    def landing(inside, inside_beside):
        return jnp.where(mine & inside, change, 0.0) + jnp.where(theirs & inside_beside, arrived, 0.0)

    arrived = send(change, BOTH, device_pairs(scatter_pairs))
    total = sum_kept + send(sum_away, "pos", swap_cores)
    total = scatter_sum(total, "pos", ring_z)
    total, arrived = lax.optimization_barrier((total, arrived))
    total, outward = lax.optimization_barrier((total, landing(cols < o1, cols < o1_beside)))
    landed = send(outward, "pos", to_right)
    total = scatter_sum(total, "readout", ring_y)
    first, second, third = around(total, "readout", ring_x)
    total = (total + second) + (first + third)
    start = flip * half + z * (SIDE // 8) + y * STRIP
    piece = lax.dynamic_slice_in_dim(probe, start, STRIP, 1) + total[:2] / total[2:]
    strips = jnp.stack([piece] + around(piece, "readout", ring_y))
    change, arrived, _ = lax.optimization_barrier((change, arrived, strips))
    inward = object_field + landing(cols >= o1, cols >= o1_beside)
    own = [strips] + around(strips, "pos", ring_z)
    own, landed, inward = lax.optimization_barrier((own, landed, inward))
    object_new = inward + landed
    other = send(jnp.stack(own), "pos", swap_cores)
    probe_new = place_strips(own, other)
    return (object_new, probe_new)


def solution(mesh):
    in_specs = (
        P("pos", "readout", None),
        P("readout", None),
        P("readout", None),
        P("pos", None),
        P(None, "readout", "pos"),
        P(),
    )
    out_specs = (P(None, "readout", "pos"), P())
    return jax.shard_map(
        on_device, mesh=mesh, in_specs=in_specs, out_specs=out_specs, check_vma=False
    )
```

time: 214 us -> 162 us (0.76)
  starting transfers between devices: 75.2 us -> 45.9 us
  waiting for transfers between devices: 81.9 us -> 58.2 us
  Pallas kernels: 25.6 us -> 28.5 us
    ppermute x33 -> x23, waiting for transfers between devices: 81.9 us -> 51.5 us  [send(): return lax.ppermute(block, axis, route)]
    ppermute x33 -> x23, starting transfers between devices: 68.2 us -> 38.9 us  [send(): return lax.ppermute(block, axis, route)]
    all_to_all x1, waiting for transfers between devices: 0.01 us -> 6.69 us  [on_device(): lax.all_to_all(binned, 'readout', split_axis=0, concat_axis=0, tiled=True)]
    add x6 -> x8, other arithmetic: 8.63 us -> 13.6 us  [the longest x1 3.38 us: on_device(): object_new = inward + landed]
    pallas_call x0 -> x1, Pallas kernels: none -> 3.04 us  [place_strips(): pl.pallas_call(place_kernel, out_shape=jax.ShapeDtypeStruct((2, SIDE, SID...]
    concatenate x2 -> x0, other arithmetic: 2.98 us -> none  [the longest x1 1.49 us: on_device(): object_new = jnp.concatenate(news, axis=1)]
    unnamed x26 -> x23, local copies, waits for them, and re-layouts: 0.83 us -> 3.79 us
    slice x2, local copies, waits for them, and re-layouts: 4.79 us -> 2.61 us  [on_device(): chunks = [object_field[:, :CUT], object_field[:, CUT:]]]
  transfers between devices with their start and end apart: 34 -> 24, of which waited for: 15 -> 15; matrix products, arithmetic and copies ran while one was open for 9% -> 11% of each run, Pallas kernels for 5% -> 7%
where the time goes in v2:
time: 162 us; the launch traced here: 161 us
  waiting for transfers between devices  58.2 us (36%)
  starting transfers between devices  45.9 us (28%)
  Pallas kernels  28.5 us (18%)
  other arithmetic  20 us (12%)
  local copies, waits for them, and re-layouts  7.18 us (4%)
    ppermute x23, waiting for transfers between devices, send(): return lax.ppermute(block, axis, route)  51.5 us
    ppermute x23, starting transfers between devices, send(): return lax.ppermute(block, axis, route)  38.9 us
    pallas_call x1, Pallas kernels, main_call(): pl.pallas_call(main_kernel, out_shape=[jax.ShapeDtypeStruct(s, F32) for s...  14.5 us
    all_to_all x1, starting transfers between devices, on_device(): lax.all_to_all(binned, 'readout', split_axis=0, concat_axis=0, tiled=True)  7.02 us
    all_to_all x1, waiting for transfers between devices, on_device(): lax.all_to_all(binned, 'readout', split_axis=0, concat_axis=0, tiled=True)  6.69 us
    pallas_call x1, Pallas kernels, bin_frames(): pl.pallas_call(bin_kernel, out_shape=jax.ShapeDtypeStruct((ROWS, 32, SIDE...  6.63 us
    pallas_call x1, Pallas kernels, roll_probe(): pl.pallas_call(roll_kernel, out_shape=[jax.ShapeDtypeStruct((2, SIDE, SID...  4.38 us
    unnamed x23, local copies, waits for them, and re-layouts  3.79 us
  transfers between devices with their start and end apart: 24, of which 15 were waited for; matrix products, arithmetic and copies ran while one was open for 11% of the time, Pallas kernels for 7%

profile of v2, /device:TPU:1, one launch (start us, length us, event | category | flops | bytes accessed | tf_op | source)
XLA Modules:
  0.0 160.8 jit_solution(7086240422032794539)
XLA Ops:
  0.6 1.2 slice.43
  1.8 1.4 slice.42
  3.2 3.3 %collective-permute-start = (f32[2,320,512]{2,1,0:T(8,128)S(1)}, f32[2,320,512]{2,1,0:T(8,128)S(1)}, u32[]{:S(2)}, u32[]{:S(2)}) collective-permute-start(f32[2,320,512]{2,1,0:T(8,128)S(1)} %slice.42), channel_id=1, source_target_pairs={{1,0},{2,1},{3,2},{4,3},{5,4},{6,5},{7,6},{9,8},{10,9},{11,10},{12... | collective-permute-start | bytes 3932168 | tf_op jit(solution)/shard_map/ppermute | solution.py:342
  6.6 6.6 %bin_frames.1 = f32[16,32,512]{2,1,0:T(8,128)} custom-call(f32[16,64,1024]{2,1,0:T(8,128)} %frames.1, f32[64,1024]{1,0:T(8,128)} %dark.1, f32[64,1024]{1,0:T(8,128)} %gain.1, bf16[1024,512]{1,0:T(8,128)(2,1)} %constant.58.clone.pairs), custom_call_target="tpu_custom_call" | custom-call | tf_op jit(solution)/shard_map/bin_frames/pallas_call | solution.py:98
  13.2 7.0 %all-to-all-start = ((f32[16,32,512]{2,1,0:T(8,128)}), f32[16,32,512]{2,1,0:T(8,128)}, u32[]{:S(2)}, u32[]{:S(2)}) async-start(f32[16,32,512]{2,1,0:T(8,128)} %bin_frames.1), calls=%async_computation | async-start | bytes 2097152 | tf_op jit(solution)/shard_map/all_to_all | solution.py:430
  20.2 1.9 %collective-permute-start.1 = (f32[2,192,512]{2,1,0:T(8,128)S(1)}, f32[2,192,512]{2,1,0:T(8,128)}, u32[]{:S(2)}, u32[]{:S(2)}) collective-permute-start(f32[2,192,512]{2,1,0:T(8,128)S(1)} %slice.43), channel_id=1, source_target_pairs={{1,0},{2,1},{3,2},{4,3},{5,4},{6,5},{7,6},{9,8},{10,9},{11,10},{12... | collective-permute-start | bytes 2359304 | tf_op jit(solution)/shard_map/ppermute | solution.py:342
  22.2 0.6 constant_dynamic-slice_fusion.1
  22.8 0.6 iota_compare_fusion.5
  23.5 0.0 collective-permute-done.r0_hbm
  23.5 1.5 broadcast_select_fusion
  25.0 3.2 %collective-permute-start.2 = (f32[2,320,512]{2,1,0:T(8,128)}, f32[2,320,512]{2,1,0:T(8,128)}, u32[]{:S(2)}, u32[]{:S(2)}) collective-permute-start(f32[2,320,512]{2,1,0:T(8,128)} %broadcast_select_fusion), channel_id=1, source_target_pairs={{1,9},{3,11},{5,13},{7,15},{8,0},{9,17},{10,2},{11,19},{12,4},{13,... | collective-permute-start | bytes 3932168 | tf_op jit(solution)/shard_map/ppermute | solution.py:342
  28.2 5.9 %collective-permute-done.1.r1_hbm = f32[2,192,512]{2,1,0:T(8,128)} collective-permute-done((f32[2,192,512]{2,1,0:T(8,128)S(1)}, f32[2,192,512]{2,1,0:T(8,128)}, u32[]{:S(2)}, u32[]{:S(2)}) %collective-permute-start.1) | collective-permute-done | bytes 786464 | tf_op jit(solution)/shard_map/ppermute | solution.py:342
  34.0 6.7 %all-to-all-done.binned_hbm = f32[16,32,512]{2,1,0:T(8,128)} async-done(((f32[16,32,512]{2,1,0:T(8,128)}), f32[16,32,512]{2,1,0:T(8,128)}, u32[]{:S(2)}, u32[]{:S(2)}) %all-to-all-start) | async-done | bytes 1048608 | tf_op jit(solution)/shard_map/all_to_all | solution.py:430
  40.7 1.3 broadcast_select_fusion.1
  42.0 2.1 %collective-permute-start.3 = (f32[2,192,512]{2,1,0:T(8,128)S(1)}, f32[2,192,512]{2,1,0:T(8,128)S(1)}, u32[]{:S(2)}, u32[]{:S(2)}) collective-permute-start(f32[2,192,512]{2,1,0:T(8,128)S(1)} %broadcast_select_fusion.1), channel_id=1, source_target_pairs={{1,9},{3,11},{5,13},{7,15},{8,0},{9,17},{10,2},{11,19},{12,4},{13,... | collective-permute-start | bytes 2359304 | tf_op jit(solution)/shard_map/ppermute | solution.py:342
  44.1 0.7 copy.12.offsets
  44.8 4.4 %roll_probe.1 = (f32[2,512,512]{2,1,0:T(8,128)}, f32[8,128]{1,0:T(8,128)}) custom-call(s32[16,2]{1,0:T(8,128)} %copy.12.offsets, f32[2,512,512]{2,1,0:T(8,128)} %probe.1), custom_call_target="tpu_custom_call" | custom-call | flops 4194304 | bytes 67108864 | tf_op jit(solution)/shard_map/roll_probe/pallas_call | solution.py:135
  49.2 11.0 %collective-permute-done.3.n1_hbm = f32[2,192,512]{2,1,0:T(8,128)S(1)} collective-permute-done((f32[2,192,512]{2,1,0:T(8,128)S(1)}, f32[2,192,512]{2,1,0:T(8,128)S(1)}, u32[]{:S(2)}, u32[]{:S(2)}) %collective-permute-start.3) | collective-permute-done | bytes 786464 | tf_op jit(solution)/shard_map/ppermute | solution.py:342
  60.2 1.0 copy-done.10
  61.1 14.5 %phase_update.1 = (f32[2,512,512]{2,1,0:T(8,128)}, f32[4,4,3,16,512]{4,3,2,1,0:T(8,128)}, f32[4,4,3,16,512]{4,3,2,1,0:T(8,128)}) custom-call(s32[16,2]{1,0:T(8,128)} %copy.12.offsets, f32[2,512,512]{2,1,0:T(8,128)} %tile_hbm.1, f32[2,320,512]{2,1,0:T(8,128)} %copy-done.4, f32[2,192,512]{2,1,0:T(8,128)} %collective-permute-done.1.r1_hbm, ...), custom_call_target="tpu_custom_call" | custom-call | flops 8589934592 | bytes 20971520 | tf_op jit(solution)/shard_map/phase_update/pallas_call | solution.py:314
  75.6 0.1 collective-permute-start.4
  75.7 5.0 %collective-permute-start.8 = (f32[2,512,512]{2,1,0:T(8,128)}, f32[2,512,512]{2,1,0:T(8,128)}, u32[]{:S(2)}, u32[]{:S(2)}) collective-permute-start(f32[2,512,512]{2,1,0:T(8,128)} %get-tuple-element.36), channel_id=1, source_target_pairs={{0,8},{1,121},{2,10},{3,123},{4,12},{5,125},{6,14},{7,127},{8,16},... | collective-permute-start | bytes 6291464 | tf_op jit(solution)/shard_map/ppermute | solution.py:342
  80.7 1.8 %add.80 = f32[4,4,3,16,512]{4,3,2,1,0:T(8,128)S(1)} add(f32[4,4,3,16,512]{4,3,2,1,0:T(8,128)} %get-tuple-element.29, f32[4,4,3,16,512]{4,3,2,1,0:T(8,128)S(1)} %collective-permute-done.4) | non-fusion elementwise | flops 393216 | bytes 4718592 | tf_op jit(solution)/shard_map/add | solution.py:450
  82.5 0.0 copy-start.2
  82.5 1.1 copy-done.2
  83.6 0.1 slice_bitcast_fusion
  83.7 2.4 %collective-permute-start.7 = (f32[4,3,16,512]{3,2,1,0:T(8,128)S(1)}, f32[4,3,16,512]{3,2,1,0:T(8,128)}, u32[]{:S(2)}, u32[]{:S(2)}) collective-permute-start(f32[4,3,16,512]{3,2,1,0:T(8,128)S(1)} %get-tuple-element.44), channel_id=1, source_target_pairs={{0,6},{1,7},{2,0},{3,1},{4,2},{5,3},{6,4},{7,5},{8,14},{9,15},{10,... | collective-permute-start | bytes 1179656 | tf_op jit(solution)/shard_map/ppermute | solution.py:342
  86.1 1.3 collective-permute-start.5
  87.4 1.2 iota_compare_fusion.1
  88.6 1.1 fusion.8
  89.7 13.0 %collective-permute-done.7 = f32[4,3,16,512]{3,2,1,0:T(8,128)} collective-permute-done((f32[4,3,16,512]{3,2,1,0:T(8,128)S(1)}, f32[4,3,16,512]{3,2,1,0:T(8,128)}, u32[]{:S(2)}, u32[]{:S(2)}) %collective-permute-start.7) | collective-permute-done | bytes 393248 | tf_op jit(solution)/shard_map/ppermute | solution.py:342
  102.8 3.3 %collective-permute-done.6 = f32[4,3,16,512]{3,2,1,0:T(8,128)} collective-permute-done((f32[4,3,16,512]{3,2,1,0:T(8,128)S(1)}, f32[4,3,16,512]{3,2,1,0:T(8,128)}, u32[]{:S(2)}, u32[]{:S(2)}) %collective-permute-start.6) | collective-permute-done | bytes 393248 | tf_op jit(solution)/shard_map/ppermute | solution.py:342
  106.1 0.0 collective-permute-done.5
  106.1 1.5 fusion.1
  107.6 3.3 %select_add_fusion = f32[2,512,512]{2,1,0:T(8,128)} fusion(f32[2,512,512]{2,1,0:T(8,128)} %collective-permute-done.8, f32[2,512,512]{2,1,0:T(8,128)S(1)} %copy-done.1, pred[512]{0:T(512)(128)(4,1)S(1)} %get-tuple-element.56, pred[512]{0:T(512)(128)(4,1)S(1)} %get-tuple-element.57, pred[512]{0:T(512)(128)(4,1)S(1)} %get-tuple-element.55, ...), kind=kLoop, calls=%fused_computation.1 | loop fusion | flops 2621440 | bytes 6293504 | tf_op jit(solution)/shard_map/add | solution.py:447
  111.0 2.0 %collective-permute-start.21 = (f32[2,512,512]{2,1,0:T(8,128)}, f32[2,512,512]{2,1,0:T(8,128)}, u32[]{:S(2)}, u32[]{:S(2)}) collective-permute-start(f32[2,512,512]{2,1,0:T(8,128)} %select_add_fusion), channel_id=1, source_target_pairs={{0,1},{1,2},{2,3},{3,4},{4,5},{5,6},{6,7},{8,9},{9,10},{10,11},{11... | collective-permute-start | bytes 6291464 | tf_op jit(solution)/shard_map/ppermute | solution.py:342
  113.0 2.0 %collective-permute-start.11 = (f32[3,16,512]{2,1,0:T(8,128)S(1)}, f32[3,16,512]{2,1,0:T(8,128)S(1)}, u32[]{:S(2)}, u32[]{:S(2)}) collective-permute-start(f32[3,16,512]{2,1,0:T(8,128)S(1)} %get-tuple-element.47), channel_id=1, source_target_pairs={{0,96},{8,104},{16,112},{24,120},{32,0},{40,8},{48,16},{56,24},{64... | collective-permute-start | bytes 294920 | tf_op jit(solution)/shard_map/ppermute | solution.py:342
  115.1 1.5 collective-permute-start.9
  116.6 0.1 collective-permute-done.11
  116.7 4.1 %collective-permute-done.10 = f32[3,16,512]{2,1,0:T(8,128)S(1)} collective-permute-done((f32[3,16,512]{2,1,0:T(8,128)S(1)}, f32[3,16,512]{2,1,0:T(8,128)S(1)}, u32[]{:S(2)}, u32[]{:S(2)}) %collective-permute-start.10) | collective-permute-done | bytes 98336 | tf_op jit(solution)/shard_map/ppermute | solution.py:342
  120.9 0.1 collective-permute-start.14
  120.9 1.5 collective-permute-start.13
  122.4 0.6 collective-permute-start.12
  123.0 1.4 collective-permute-done.14
  124.4 1.3 collective-permute-done.13
  125.7 1.7 %collective-permute-done.12 = f32[3,16,512]{2,1,0:T(8,128)S(1)} collective-permute-done((f32[3,16,512]{2,1,0:T(8,128)S(1)}, f32[3,16,512]{2,1,0:T(8,128)S(1)}, u32[]{:S(2)}, u32[]{:S(2)}) %collective-permute-start.12) | collective-permute-done | bytes 98336 | tf_op jit(solution)/shard_map/ppermute | solution.py:342
  127.4 0.9 fusion.3
  128.3 2.1 %collective-permute-start.17 = (f32[2,16,512]{2,1,0:T(8,128)S(1)}, f32[2,16,512]{2,1,0:T(8,128)S(1)}, u32[]{:S(2)}, u32[]{:S(2)}) collective-permute-start(f32[2,16,512]{2,1,0:T(8,128)S(1)} %fusion.3), channel_id=1, source_target_pairs={{0,96},{8,104},{16,112},{24,120},{32,0},{40,8},{48,16},{56,24},{64... | collective-permute-start | bytes 196616 | tf_op jit(solution)/shard_map/ppermute | solution.py:342
  130.4 0.3 collective-permute-start.16
  130.7 0.4 collective-permute-start.15
  131.0 0.6 iota_compare_fusion
  131.7 0.6 collective-permute-done.17
  132.3 2.8 %collective-permute-done.16 = f32[2,16,512]{2,1,0:T(8,128)S(1)} collective-permute-done((f32[2,16,512]{2,1,0:T(8,128)S(1)}, f32[2,16,512]{2,1,0:T(8,128)S(1)}, u32[]{:S(2)}, u32[]{:S(2)}) %collective-permute-start.16) | collective-permute-done | bytes 65568 | tf_op jit(solution)/shard_map/ppermute | solution.py:342
  135.1 0.6 collective-permute-done.15
  135.7 0.3 collective-permute-start.20
  136.0 4.3 %collective-permute-start.19 = (f32[4,2,16,512]{3,2,1,0:T(8,128)S(1)}, f32[4,2,16,512]{3,2,1,0:T(8,128)S(1)}, u32[]{:S(2)}, u32[]{:S(2)}) collective-permute-start(f32[4,2,16,512]{3,2,1,0:T(8,128)S(1)} %pad_maximum_fusion.1.o0), channel_id=1, source_target_pairs={{0,4},{1,5},{2,6},{3,7},{4,0},{5,1},{6,2},{7,3},{8,12},{9,13},{10,... | collective-permute-start | bytes 786440 | tf_op jit(solution)/shard_map/ppermute | solution.py:342
  140.4 2.7 %add_add_fusion = f32[2,512,512]{2,1,0:T(8,128)S(1)} fusion(f32[2,512,512]{2,1,0:T(8,128)S(1)} %copy-done, f32[2,512,512]{2,1,0:T(8,128)} %collective-permute-done.8, f32[2,512,512]{2,1,0:T(8,128)} %get-tuple-element.36, pred[512]{0:T(512)(128)(4,1)S(1)} %iota_compare_fusion.5, pred[512]{0:T(512)(128)(4,1)S(1)} %iota_compare_fusion, ...), kind=kLoop, calls=%fused_computation | loop fusion | flops 3145728 | bytes 8390656 | tf_op jit(solution)/shard_map/add | solution.py:462
  143.1 1.0 collective-permute-done.19.o2
  144.1 4.6 %collective-permute-done.18.o1 = f32[4,2,16,512]{3,2,1,0:T(8,128)S(1)} collective-permute-done((f32[4,2,16,512]{3,2,1,0:T(8,128)S(1)}, f32[4,2,16,512]{3,2,1,0:T(8,128)S(1)}, u32[]{:S(2)}, u32[]{:S(2)}) %collective-permute-start.18) | collective-permute-done | bytes 262176 | tf_op jit(solution)/shard_map/ppermute | solution.py:342
  148.7 0.1 pad_maximum_fusion
  148.8 4.6 %collective-permute-start.22 = (f32[4,4,2,16,512]{4,3,2,1,0:T(8,128)S(1)}, f32[4,4,2,16,512]{4,3,2,1,0:T(8,128)S(1)}, u32[]{:S(2)}, u32[]{:S(2)}) collective-permute-start(f32[4,4,2,16,512]{4,3,2,1,0:T(8,128)S(1)} %pad_maximum_fusion), channel_id=1, source_target_pairs={{0,1},{1,0},{2,3},{3,2},{4,5},{5,4},{6,7},{7,6},{8,9},{9,8},{10,11... | collective-permute-start | bytes 3145736 | tf_op jit(solution)/shard_map/ppermute | solution.py:342
  153.4 3.4 %add.96 = f32[2,512,512]{2,1,0:T(8,128)} add(f32[2,512,512]{2,1,0:T(8,128)S(1)} %add_add_fusion, f32[2,512,512]{2,1,0:T(8,128)} %collective-permute-done.21) | non-fusion elementwise | flops 524288 | bytes 6291456 | tf_op jit(solution)/shard_map/add | solution.py:465
  156.8 1.0 copy-done.5
  157.8 3.0 %place_strips.1 = f32[2,512,512]{2,1,0:T(8,128)} custom-call(f32[4,2,16,512]{3,2,1,0:T(8,128)} %copy-done.3, f32[4,2,16,512]{3,2,1,0:T(8,128)} %copy-done.8, f32[4,2,16,512]{3,2,1,0:T(8,128)} %copy-done.7, f32[4,2,16,512]{3,2,1,0:T(8,128)} %copy-done.6, f32[4,4,2,16,512]{4,3,2,1,0:T(8,128)} %copy-done.5), custom_call_target="tpu_custom_call" | custom-call | bytes 4194304 | tf_op jit(solution)/shard_map/place_strips/pallas_call | solution.py:399
  (33 shorter events, 0.2 us)
Async XLA Ops:
  3.2 20.2 %collective-permute-start = (f32[2,320,512]{2,1,0:T(8,128)S(1)}, f32[2,320,512]{2,1,0:T(8,128)S(1)}, u32[]{:S(2)}, u32[]{:S(2)}) collective-permute-start(f32[2,320,512]{2,1,0:T(8,128)S(1)} %slice.42), channel_id=1, source_target_pairs={{1,0},{2,1},{3,2},{4,3},{5,4},{6,5},{7,6},{9,8},{10,9},{11,10},{12... | collective-permute-start | bytes 3932168 | tf_op jit(solution)/shard_map/ppermute | solution.py:342
  13.2 9.0 %copy-start.9 = (s32[16,2]{0,1:T(2,128)S(1)}, s32[16,2]{0,1:T(2,128)}, u32[]{:S(2)}) copy-start(s32[16,2]{0,1:T(2,128)} %param.12) | copy-start | bytes 388
  13.2 27.5 %all-to-all-start = ((f32[16,32,512]{2,1,0:T(8,128)}), f32[16,32,512]{2,1,0:T(8,128)}, u32[]{:S(2)}, u32[]{:S(2)}) async-start(f32[16,32,512]{2,1,0:T(8,128)} %bin_frames.1), calls=%async_computation | async-start | bytes 2097152 | tf_op jit(solution)/shard_map/all_to_all | solution.py:430
  20.2 13.8 %collective-permute-start.1 = (f32[2,192,512]{2,1,0:T(8,128)S(1)}, f32[2,192,512]{2,1,0:T(8,128)}, u32[]{:S(2)}, u32[]{:S(2)}) collective-permute-start(f32[2,192,512]{2,1,0:T(8,128)S(1)} %slice.43), channel_id=1, source_target_pairs={{1,0},{2,1},{3,2},{4,3},{5,4},{6,5},{7,6},{9,8},{10,9},{11,10},{12... | collective-permute-start | bytes 2359304 | tf_op jit(solution)/shard_map/ppermute | solution.py:342
  23.5 18.5 %copy-start.4 = (f32[2,320,512]{2,1,0:T(8,128)}, f32[2,320,512]{2,1,0:T(8,128)S(1)}, u32[]{:S(2)}) copy-start(f32[2,320,512]{2,1,0:T(8,128)S(1)} %collective-permute-done.r0_hbm) | copy-start | bytes 3932164
  25.0 35.2 %collective-permute-start.2 = (f32[2,320,512]{2,1,0:T(8,128)}, f32[2,320,512]{2,1,0:T(8,128)}, u32[]{:S(2)}, u32[]{:S(2)}) collective-permute-start(f32[2,320,512]{2,1,0:T(8,128)} %broadcast_select_fusion), channel_id=1, source_target_pairs={{1,9},{3,11},{5,13},{7,15},{8,0},{9,17},{10,2},{11,19},{12,4},{13,... | collective-permute-start | bytes 3932168 | tf_op jit(solution)/shard_map/ppermute | solution.py:342
  42.0 18.2 %collective-permute-start.3 = (f32[2,192,512]{2,1,0:T(8,128)S(1)}, f32[2,192,512]{2,1,0:T(8,128)S(1)}, u32[]{:S(2)}, u32[]{:S(2)}) collective-permute-start(f32[2,192,512]{2,1,0:T(8,128)S(1)} %broadcast_select_fusion.1), channel_id=1, source_target_pairs={{1,9},{3,11},{5,13},{7,15},{8,0},{9,17},{10,2},{11,19},{12,4},{13,... | collective-permute-start | bytes 2359304 | tf_op jit(solution)/shard_map/ppermute | solution.py:342
  60.2 1.0 copy-start.10
  75.6 5.1 %collective-permute-start.4 = (f32[4,4,3,16,512]{4,3,2,1,0:T(8,128)}, f32[4,4,3,16,512]{4,3,2,1,0:T(8,128)S(1)}, u32[]{:S(2)}, u32[]{:S(2)}) collective-permute-start(f32[4,4,3,16,512]{4,3,2,1,0:T(8,128)} %get-tuple-element.30), channel_id=1, source_target_pairs={{0,1},{1,0},{2,3},{3,2},{4,5},{5,4},{6,7},{7,6},{8,9},{9,8},{10,11... | collective-permute-start | bytes 4718600 | tf_op jit(solution)/shard_map/ppermute | solution.py:342
  75.7 31.9 %collective-permute-start.8 = (f32[2,512,512]{2,1,0:T(8,128)}, f32[2,512,512]{2,1,0:T(8,128)}, u32[]{:S(2)}, u32[]{:S(2)}) collective-permute-start(f32[2,512,512]{2,1,0:T(8,128)} %get-tuple-element.36), channel_id=1, source_target_pairs={{0,8},{1,121},{2,10},{3,123},{4,12},{5,125},{6,14},{7,127},{8,16},... | collective-permute-start | bytes 6291464 | tf_op jit(solution)/shard_map/ppermute | solution.py:342
  82.5 1.1 copy-start.2
  83.6 24.0 %copy-start.1 = (f32[2,512,512]{2,1,0:T(8,128)S(1)}, f32[2,512,512]{2,1,0:T(8,128)}, u32[]{:S(2)}) copy-start(f32[2,512,512]{2,1,0:T(8,128)} %get-tuple-element.36) | copy-start | bytes 6291460
  83.7 19.0 %collective-permute-start.7 = (f32[4,3,16,512]{3,2,1,0:T(8,128)S(1)}, f32[4,3,16,512]{3,2,1,0:T(8,128)}, u32[]{:S(2)}, u32[]{:S(2)}) collective-permute-start(f32[4,3,16,512]{3,2,1,0:T(8,128)S(1)} %get-tuple-element.44), channel_id=1, source_target_pairs={{0,6},{1,7},{2,0},{3,1},{4,2},{5,3},{6,4},{7,5},{8,14},{9,15},{10,... | collective-permute-start | bytes 1179656 | tf_op jit(solution)/shard_map/ppermute | solution.py:342
  86.1 20.0 %collective-permute-start.6 = (f32[4,3,16,512]{3,2,1,0:T(8,128)S(1)}, f32[4,3,16,512]{3,2,1,0:T(8,128)}, u32[]{:S(2)}, u32[]{:S(2)}) collective-permute-start(f32[4,3,16,512]{3,2,1,0:T(8,128)S(1)} %get-tuple-element.45), channel_id=1, source_target_pairs={{0,2},{1,3},{2,4},{3,5},{4,6},{5,7},{6,0},{7,1},{8,10},{9,11},{10,... | collective-permute-start | bytes 1179656 | tf_op jit(solution)/shard_map/ppermute | solution.py:342
  86.1 20.0 %collective-permute-start.5 = (f32[4,3,16,512]{3,2,1,0:T(8,128)S(1)}, f32[4,3,16,512]{3,2,1,0:T(8,128)}, u32[]{:S(2)}, u32[]{:S(2)}) collective-permute-start(f32[4,3,16,512]{3,2,1,0:T(8,128)S(1)} %get-tuple-element.46), channel_id=1, source_target_pairs={{0,4},{1,5},{2,6},{3,7},{4,0},{5,1},{6,2},{7,3},{8,12},{9,13},{10,... | collective-permute-start | bytes 1179656 | tf_op jit(solution)/shard_map/ppermute | solution.py:342
  111.0 29.4 %copy-start = (f32[2,512,512]{2,1,0:T(8,128)S(1)}, f32[2,512,512]{2,1,0:T(8,128)}, u32[]{:S(2)}) copy-start(f32[2,512,512]{2,1,0:T(8,128)} %tile_hbm.1) | copy-start | bytes 6291460
  111.0 37.7 %collective-permute-start.21 = (f32[2,512,512]{2,1,0:T(8,128)}, f32[2,512,512]{2,1,0:T(8,128)}, u32[]{:S(2)}, u32[]{:S(2)}) collective-permute-start(f32[2,512,512]{2,1,0:T(8,128)} %select_add_fusion), channel_id=1, source_target_pairs={{0,1},{1,2},{2,3},{3,4},{4,5},{5,6},{6,7},{8,9},{9,10},{10,11},{11... | collective-permute-start | bytes 6291464 | tf_op jit(solution)/shard_map/ppermute | solution.py:342
  113.0 3.7 %collective-permute-start.11 = (f32[3,16,512]{2,1,0:T(8,128)S(1)}, f32[3,16,512]{2,1,0:T(8,128)S(1)}, u32[]{:S(2)}, u32[]{:S(2)}) collective-permute-start(f32[3,16,512]{2,1,0:T(8,128)S(1)} %get-tuple-element.47), channel_id=1, source_target_pairs={{0,96},{8,104},{16,112},{24,120},{32,0},{40,8},{48,16},{56,24},{64... | collective-permute-start | bytes 294920 | tf_op jit(solution)/shard_map/ppermute | solution.py:342
  115.1 5.7 %collective-permute-start.10 = (f32[3,16,512]{2,1,0:T(8,128)S(1)}, f32[3,16,512]{2,1,0:T(8,128)S(1)}, u32[]{:S(2)}, u32[]{:S(2)}) collective-permute-start(f32[3,16,512]{2,1,0:T(8,128)S(1)} %get-tuple-element.48), channel_id=1, source_target_pairs={{0,32},{8,40},{16,48},{24,56},{32,64},{40,72},{48,80},{56,88},{64,... | collective-permute-start | bytes 294920 | tf_op jit(solution)/shard_map/ppermute | solution.py:342
  115.1 5.7 %collective-permute-start.9 = (f32[3,16,512]{2,1,0:T(8,128)S(1)}, f32[3,16,512]{2,1,0:T(8,128)S(1)}, u32[]{:S(2)}, u32[]{:S(2)}) collective-permute-start(f32[3,16,512]{2,1,0:T(8,128)S(1)} %get-tuple-element.49), channel_id=1, source_target_pairs={{0,64},{8,72},{16,80},{24,88},{32,96},{40,104},{48,112},{56,120},{... | collective-permute-start | bytes 294920 | tf_op jit(solution)/shard_map/ppermute | solution.py:342
  120.9 3.5 %collective-permute-start.14 = (f32[3,16,512]{2,1,0:T(8,128)S(1)}, f32[3,16,512]{2,1,0:T(8,128)S(1)}, u32[]{:S(2)}, u32[]{:S(2)}) collective-permute-start(f32[3,16,512]{2,1,0:T(8,128)S(1)} %fusion.2), channel_id=1, source_target_pairs={{0,24},{8,0},{16,8},{24,16},{32,56},{40,32},{48,40},{56,48},{64,88... | collective-permute-start | bytes 294920 | tf_op jit(solution)/shard_map/ppermute | solution.py:342
  120.9 4.7 %collective-permute-start.13 = (f32[3,16,512]{2,1,0:T(8,128)S(1)}, f32[3,16,512]{2,1,0:T(8,128)S(1)}, u32[]{:S(2)}, u32[]{:S(2)}) collective-permute-start(f32[3,16,512]{2,1,0:T(8,128)S(1)} %fusion.2), channel_id=1, source_target_pairs={{0,8},{8,16},{16,24},{24,0},{32,40},{40,48},{48,56},{56,32},{64,72... | collective-permute-start | bytes 294920 | tf_op jit(solution)/shard_map/ppermute | solution.py:342
  122.4 5.0 %collective-permute-start.12 = (f32[3,16,512]{2,1,0:T(8,128)S(1)}, f32[3,16,512]{2,1,0:T(8,128)S(1)}, u32[]{:S(2)}, u32[]{:S(2)}) collective-permute-start(f32[3,16,512]{2,1,0:T(8,128)S(1)} %fusion.2), channel_id=1, source_target_pairs={{0,16},{8,24},{16,0},{24,8},{32,48},{40,56},{48,32},{56,40},{64,80... | collective-permute-start | bytes 294920 | tf_op jit(solution)/shard_map/ppermute | solution.py:342
  128.3 4.0 %collective-permute-start.17 = (f32[2,16,512]{2,1,0:T(8,128)S(1)}, f32[2,16,512]{2,1,0:T(8,128)S(1)}, u32[]{:S(2)}, u32[]{:S(2)}) collective-permute-start(f32[2,16,512]{2,1,0:T(8,128)S(1)} %fusion.3), channel_id=1, source_target_pairs={{0,96},{8,104},{16,112},{24,120},{32,0},{40,8},{48,16},{56,24},{64... | collective-permute-start | bytes 196616 | tf_op jit(solution)/shard_map/ppermute | solution.py:342
  130.4 4.7 %collective-permute-start.16 = (f32[2,16,512]{2,1,0:T(8,128)S(1)}, f32[2,16,512]{2,1,0:T(8,128)S(1)}, u32[]{:S(2)}, u32[]{:S(2)}) collective-permute-start(f32[2,16,512]{2,1,0:T(8,128)S(1)} %fusion.3), channel_id=1, source_target_pairs={{0,64},{8,72},{16,80},{24,88},{32,96},{40,104},{48,112},{56,120},{... | collective-permute-start | bytes 196616 | tf_op jit(solution)/shard_map/ppermute | solution.py:342
  130.7 5.0 %collective-permute-start.15 = (f32[2,16,512]{2,1,0:T(8,128)S(1)}, f32[2,16,512]{2,1,0:T(8,128)S(1)}, u32[]{:S(2)}, u32[]{:S(2)}) collective-permute-start(f32[2,16,512]{2,1,0:T(8,128)S(1)} %fusion.3), channel_id=1, source_target_pairs={{0,32},{8,40},{16,48},{24,56},{32,64},{40,72},{48,80},{56,88},{64,... | collective-permute-start | bytes 196616 | tf_op jit(solution)/shard_map/ppermute | solution.py:342
  135.7 13.0 %copy-start.3 = (f32[4,2,16,512]{3,2,1,0:T(8,128)}, f32[4,2,16,512]{3,2,1,0:T(8,128)S(1)}, u32[]{:S(2)}) copy-start(f32[4,2,16,512]{3,2,1,0:T(8,128)S(1)} %pad_maximum_fusion.1.o0) | copy-start | bytes 786436
  135.7 7.3 %collective-permute-start.20 = (f32[4,2,16,512]{3,2,1,0:T(8,128)S(1)}, f32[4,2,16,512]{3,2,1,0:T(8,128)S(1)}, u32[]{:S(2)}, u32[]{:S(2)}) collective-permute-start(f32[4,2,16,512]{3,2,1,0:T(8,128)S(1)} %pad_maximum_fusion.1.o0), channel_id=1, source_target_pairs={{0,6},{1,7},{2,0},{3,1},{4,2},{5,3},{6,4},{7,5},{8,14},{9,15},{10,... | collective-permute-start | bytes 786440 | tf_op jit(solution)/shard_map/ppermute | solution.py:342
  136.0 8.1 %collective-permute-start.19 = (f32[4,2,16,512]{3,2,1,0:T(8,128)S(1)}, f32[4,2,16,512]{3,2,1,0:T(8,128)S(1)}, u32[]{:S(2)}, u32[]{:S(2)}) collective-permute-start(f32[4,2,16,512]{3,2,1,0:T(8,128)S(1)} %pad_maximum_fusion.1.o0), channel_id=1, source_target_pairs={{0,4},{1,5},{2,6},{3,7},{4,0},{5,1},{6,2},{7,3},{8,12},{9,13},{10,... | collective-permute-start | bytes 786440 | tf_op jit(solution)/shard_map/ppermute | solution.py:342
  140.3 8.3 %collective-permute-start.18 = (f32[4,2,16,512]{3,2,1,0:T(8,128)S(1)}, f32[4,2,16,512]{3,2,1,0:T(8,128)S(1)}, u32[]{:S(2)}, u32[]{:S(2)}) collective-permute-start(f32[4,2,16,512]{3,2,1,0:T(8,128)S(1)} %pad_maximum_fusion.1.o0), channel_id=1, source_target_pairs={{0,2},{1,3},{2,4},{3,5},{4,6},{5,7},{6,0},{7,1},{8,10},{9,11},{10,... | collective-permute-start | bytes 786440 | tf_op jit(solution)/shard_map/ppermute | solution.py:342
  143.1 13.7 %copy-start.6 = (f32[4,2,16,512]{3,2,1,0:T(8,128)}, f32[4,2,16,512]{3,2,1,0:T(8,128)S(1)}, u32[]{:S(2)}) copy-start(f32[4,2,16,512]{3,2,1,0:T(8,128)S(1)} %collective-permute-done.20.o3) | copy-start | bytes 786436
  144.1 12.7 %copy-start.7 = (f32[4,2,16,512]{3,2,1,0:T(8,128)}, f32[4,2,16,512]{3,2,1,0:T(8,128)S(1)}, u32[]{:S(2)}) copy-start(f32[4,2,16,512]{3,2,1,0:T(8,128)S(1)} %collective-permute-done.19.o2) | copy-start | bytes 786436
  148.7 8.1 %copy-start.8 = (f32[4,2,16,512]{3,2,1,0:T(8,128)}, f32[4,2,16,512]{3,2,1,0:T(8,128)S(1)}, u32[]{:S(2)}) copy-start(f32[4,2,16,512]{3,2,1,0:T(8,128)S(1)} %collective-permute-done.18.o1) | copy-start | bytes 786436
  148.8 8.0 %collective-permute-start.22 = (f32[4,4,2,16,512]{4,3,2,1,0:T(8,128)S(1)}, f32[4,4,2,16,512]{4,3,2,1,0:T(8,128)S(1)}, u32[]{:S(2)}, u32[]{:S(2)}) collective-permute-start(f32[4,4,2,16,512]{4,3,2,1,0:T(8,128)S(1)} %pad_maximum_fusion), channel_id=1, source_target_pairs={{0,1},{1,0},{2,3},{3,2},{4,5},{5,4},{6,7},{7,6},{8,9},{9,8},{10,11... | collective-permute-start | bytes 3145736 | tf_op jit(solution)/shard_map/ppermute | solution.py:342
  156.8 1.0 copy-start.5

commit v3 on v2

--- a/solution.py
+++ b/solution.py
@@ -80,13 +80,9 @@
                 first = 32 * n + 8 * group
                 sums[first : first + 8, QUARTER * t : QUARTER * (t + 1)] = total
     values = sums[...]
-    high = values.astype(BF16)
-    rest = values - high.astype(F32)
-    mid = rest.astype(BF16)
-    low = (rest - mid.astype(F32)).astype(BF16)
+    high, low = split_two(values)
     table = pairs[...]
     binned = jnp.dot(low, table, preferred_element_type=F32)
-    binned += jnp.dot(mid, table, preferred_element_type=F32)
     binned += jnp.dot(high, table, preferred_element_type=F32)
     for n in range(count):
         place = lax.rem(step * count + n + flip, ROWS)
@@ -385,26 +381,35 @@
     return (values[0] + second) + (first + third)
 
 
-def place_kernel(o0, o1, o2, o3, other, out):
+def place_kernel(mine, *refs):
     _, _, y, z, core = my_place()
-    for i, own in enumerate((o0, o1, o2, o3)):
+    pieces, out, rows, sem = refs[:4], refs[-3], refs[-2], refs[-1]
+    half = core if mine else 1 - core
+    for i in range(4):
         for j in range(4):
+            strip = strip_rows(0, z + 4 - i, y + 4 - j)
             for part in range(2):
-                out[part, strip_rows(core, z + 4 - i, y + 4 - j), :] = own[j, part]
-                out[part, strip_rows(1 - core, z + 4 - i, y + 4 - j), :] = other[i, j, part]
-
-
-def place_strips(own, other):
+                rows[part, strip, :] = pieces[i][j, part] if mine else refs[0][i, j, part]
+    target = out.at[:, pl.ds(pl.multiple_of(half * (SIDE // 2), SIDE // 2), SIDE // 2), :]
+    copy = pltpu.make_async_copy(rows, target, sem)
+    copy.start()
+    copy.wait()
+
+
+def place_strips(mine, arrays):
+    anywhere = pl.BlockSpec(memory_space=pl.ANY)
     vmem = pl.BlockSpec(memory_space=pltpu.VMEM)
     return pl.pallas_call(
-        place_kernel,
+        functools.partial(place_kernel, mine),
         out_shape=jax.ShapeDtypeStruct((2, SIDE, SIDE), F32),
-        in_specs=[vmem] * 5,
-        out_specs=vmem,
+        in_specs=[vmem] * 4 if mine else [vmem, anywhere],
+        out_specs=anywhere,
+        input_output_aliases={} if mine else {1: 0},
+        scratch_shapes=[pltpu.VMEM((2, SIDE // 2, SIDE), F32), pltpu.SemaphoreType.DMA(())],
         compiler_params=pltpu.CompilerParams(vmem_limit_bytes=VMEM_BYTES),
-        cost_estimate=pl.CostEstimate(flops=0, bytes_accessed=4 * 2**20, transcendentals=0),
-        name="place_strips",
-    )(*own, other)
+        cost_estimate=pl.CostEstimate(flops=0, bytes_accessed=2 * 2**20, transcendentals=0),
+        name="place_mine" if mine else "place_other",
+    )(*arrays)
 
 
 def on_device(frames, dark, gain, offsets, object_field, probe):
@@ -461,10 +466,10 @@
     change, arrived, _ = lax.optimization_barrier((change, arrived, strips))
     inward = object_field + landing(cols >= o1, cols >= o1_beside)
     own = [strips] + around(strips, "pos", ring_z)
-    own, landed, inward = lax.optimization_barrier((own, landed, inward))
     object_new = inward + landed
+    own, object_new = lax.optimization_barrier((own, object_new))
     other = send(jnp.stack(own), "pos", swap_cores)
-    probe_new = place_strips(own, other)
+    probe_new = place_strips(False, [other, place_strips(True, own)])
     return (object_new, probe_new)
 
 

time: 162 us -> 159 us (0.981)
  waiting for transfers between devices: 58.2 us -> 56.4 us
    add x1 -> x0, other arithmetic: 2.7 us -> none  [on_device(): inward = object_field + landing(cols >= o1, cols >= o1_beside)]
    ppermute x23, waiting for transfers between devices: 51.5 us -> 49.6 us  [send(): return lax.ppermute(block, axis, route)]
    pallas_call x1 -> x2, Pallas kernels: 3.04 us -> 4.54 us  [place_strips(): pl.pallas_call(functools.partial(place_kernel, mine), out_shape=jax.Shape...]
  transfers between devices with their start and end apart: 24 -> 24, of which waited for: 15 -> 15; matrix products, arithmetic and copies ran while one was open for 11% -> 11% of each run, Pallas kernels for 7% -> 8%
where the time goes in v3:
time: 159 us
  waiting for transfers between devices  56.4 us (35%)
  starting transfers between devices  45.8 us (29%)
  Pallas kernels  29.4 us (18%)
  other arithmetic  18.7 us (12%)
  local copies, waits for them, and re-layouts  7.19 us (5%)
    ppermute x23, waiting for transfers between devices, send(): return lax.ppermute(block, axis, route)  49.6 us
    ppermute x23, starting transfers between devices, send(): return lax.ppermute(block, axis, route)  38.7 us
    pallas_call x1, Pallas kernels, main_call(): pl.pallas_call(main_kernel, out_shape=[jax.ShapeDtypeStruct(s, F32) for s...  14.5 us
    all_to_all x1, starting transfers between devices, on_device(): lax.all_to_all(binned, 'readout', split_axis=0, concat_axis=0, tiled=True)  7.02 us
    all_to_all x1, waiting for transfers between devices, on_device(): lax.all_to_all(binned, 'readout', split_axis=0, concat_axis=0, tiled=True)  6.76 us
    pallas_call x1, Pallas kernels, bin_frames(): pl.pallas_call(bin_kernel, out_shape=jax.ShapeDtypeStruct((ROWS, 32, SIDE...  5.99 us
    add x1, other arithmetic, on_device(): object_new = inward + landed  4.74 us
    pallas_call x2, Pallas kernels, place_strips(): pl.pallas_call(functools.partial(place_kernel, mine), out_shape=jax.Shape...  4.54 us
  transfers between devices with their start and end apart: 24, of which 15 were waited for; matrix products, arithmetic and copies ran while one was open for 11% of the time, Pallas kernels for 8%

profile of v3, /device:TPU:1, one launch (start us, length us, event | category | flops | bytes accessed | tf_op | source)
XLA Modules:
  0.0 158.5 jit_solution(11546339125251322304)
XLA Ops:
  0.6 1.2 slice.43
  1.8 1.4 slice.42
  3.2 3.3 %collective-permute-start = (f32[2,320,512]{2,1,0:T(8,128)S(1)}, f32[2,320,512]{2,1,0:T(8,128)S(1)}, u32[]{:S(2)}, u32[]{:S(2)}) collective-permute-start(f32[2,320,512]{2,1,0:T(8,128)S(1)} %slice.42), channel_id=1, source_target_pairs={{1,0},{2,1},{3,2},{4,3},{5,4},{6,5},{7,6},{9,8},{10,9},{11,10},{12... | collective-permute-start | bytes 3932168 | tf_op jit(solution)/shard_map/ppermute | solution.py:338
  6.6 6.0 %bin_frames.1 = f32[16,32,512]{2,1,0:T(8,128)} custom-call(f32[16,64,1024]{2,1,0:T(8,128)} %frames.1, f32[64,1024]{1,0:T(8,128)} %dark.1, f32[64,1024]{1,0:T(8,128)} %gain.1, bf16[1024,512]{1,0:T(8,128)(2,1)} %constant.58.clone.pairs), custom_call_target="tpu_custom_call" | custom-call | tf_op jit(solution)/shard_map/bin_frames/pallas_call | solution.py:94
  12.6 7.0 %all-to-all-start = ((f32[16,32,512]{2,1,0:T(8,128)}), f32[16,32,512]{2,1,0:T(8,128)}, u32[]{:S(2)}, u32[]{:S(2)}) async-start(f32[16,32,512]{2,1,0:T(8,128)} %bin_frames.1), calls=%async_computation | async-start | bytes 2097152 | tf_op jit(solution)/shard_map/all_to_all | solution.py:435
  19.6 1.9 %collective-permute-start.1 = (f32[2,192,512]{2,1,0:T(8,128)S(1)}, f32[2,192,512]{2,1,0:T(8,128)}, u32[]{:S(2)}, u32[]{:S(2)}) collective-permute-start(f32[2,192,512]{2,1,0:T(8,128)S(1)} %slice.43), channel_id=1, source_target_pairs={{1,0},{2,1},{3,2},{4,3},{5,4},{6,5},{7,6},{9,8},{10,9},{11,10},{12... | collective-permute-start | bytes 2359304 | tf_op jit(solution)/shard_map/ppermute | solution.py:338
  21.6 0.6 constant_dynamic-slice_fusion.1
  22.2 0.6 iota_compare_fusion.5
  22.8 1.0 collective-permute-done.r0_hbm
  23.9 1.5 broadcast_select_fusion
  25.4 3.1 %collective-permute-start.2 = (f32[2,320,512]{2,1,0:T(8,128)}, f32[2,320,512]{2,1,0:T(8,128)}, u32[]{:S(2)}, u32[]{:S(2)}) collective-permute-start(f32[2,320,512]{2,1,0:T(8,128)} %broadcast_select_fusion), channel_id=1, source_target_pairs={{1,9},{3,11},{5,13},{7,15},{8,0},{9,17},{10,2},{11,19},{12,4},{13,... | collective-permute-start | bytes 3932168 | tf_op jit(solution)/shard_map/ppermute | solution.py:338
  28.5 4.9 %collective-permute-done.1.r1_hbm = f32[2,192,512]{2,1,0:T(8,128)} collective-permute-done((f32[2,192,512]{2,1,0:T(8,128)S(1)}, f32[2,192,512]{2,1,0:T(8,128)}, u32[]{:S(2)}, u32[]{:S(2)}) %collective-permute-start.1) | collective-permute-done | bytes 786464 | tf_op jit(solution)/shard_map/ppermute | solution.py:338
  33.4 6.8 %all-to-all-done.binned_hbm = f32[16,32,512]{2,1,0:T(8,128)} async-done(((f32[16,32,512]{2,1,0:T(8,128)}), f32[16,32,512]{2,1,0:T(8,128)}, u32[]{:S(2)}, u32[]{:S(2)}) %all-to-all-start) | async-done | bytes 1048608 | tf_op jit(solution)/shard_map/all_to_all | solution.py:435
  40.1 1.3 broadcast_select_fusion.1
  41.4 2.1 %collective-permute-start.3 = (f32[2,192,512]{2,1,0:T(8,128)S(1)}, f32[2,192,512]{2,1,0:T(8,128)S(1)}, u32[]{:S(2)}, u32[]{:S(2)}) collective-permute-start(f32[2,192,512]{2,1,0:T(8,128)S(1)} %broadcast_select_fusion.1), channel_id=1, source_target_pairs={{1,9},{3,11},{5,13},{7,15},{8,0},{9,17},{10,2},{11,19},{12,4},{13,... | collective-permute-start | bytes 2359304 | tf_op jit(solution)/shard_map/ppermute | solution.py:338
  43.5 0.7 copy.13.offsets
  44.2 4.4 %roll_probe.1 = (f32[2,512,512]{2,1,0:T(8,128)}, f32[8,128]{1,0:T(8,128)}) custom-call(s32[16,2]{1,0:T(8,128)} %copy.13.offsets, f32[2,512,512]{2,1,0:T(8,128)} %probe.1), custom_call_target="tpu_custom_call" | custom-call | flops 4194304 | bytes 67108864 | tf_op jit(solution)/shard_map/roll_probe/pallas_call | solution.py:131
  48.6 11.0 %collective-permute-done.3.n1_hbm = f32[2,192,512]{2,1,0:T(8,128)S(1)} collective-permute-done((f32[2,192,512]{2,1,0:T(8,128)S(1)}, f32[2,192,512]{2,1,0:T(8,128)S(1)}, u32[]{:S(2)}, u32[]{:S(2)}) %collective-permute-start.3) | collective-permute-done | bytes 786464 | tf_op jit(solution)/shard_map/ppermute | solution.py:338
  59.6 0.0 collective-permute-done.2.n0_hbm
  59.6 1.0 copy-done.10
  60.5 14.5 %phase_update.1 = (f32[2,512,512]{2,1,0:T(8,128)}, f32[4,4,3,16,512]{4,3,2,1,0:T(8,128)}, f32[4,4,3,16,512]{4,3,2,1,0:T(8,128)}) custom-call(s32[16,2]{1,0:T(8,128)} %copy.13.offsets, f32[2,512,512]{2,1,0:T(8,128)} %tile_hbm.1, f32[2,320,512]{2,1,0:T(8,128)} %copy-done.4, f32[2,192,512]{2,1,0:T(8,128)} %collective-permute-done.1.r1_hbm, ...), custom_call_target="tpu_custom_call" | custom-call | flops 8589934592 | bytes 20971520 | tf_op jit(solution)/shard_map/phase_update/pallas_call | solution.py:310
  75.0 0.1 collective-permute-start.4
  75.1 5.0 %collective-permute-start.8 = (f32[2,512,512]{2,1,0:T(8,128)}, f32[2,512,512]{2,1,0:T(8,128)}, u32[]{:S(2)}, u32[]{:S(2)}) collective-permute-start(f32[2,512,512]{2,1,0:T(8,128)} %get-tuple-element.34), channel_id=1, source_target_pairs={{0,8},{1,121},{2,10},{3,123},{4,12},{5,125},{6,14},{7,127},{8,16},... | collective-permute-start | bytes 6291464 | tf_op jit(solution)/shard_map/ppermute | solution.py:338
  80.1 1.8 %add.80 = f32[4,4,3,16,512]{4,3,2,1,0:T(8,128)S(1)} add(f32[4,4,3,16,512]{4,3,2,1,0:T(8,128)} %get-tuple-element.28, f32[4,4,3,16,512]{4,3,2,1,0:T(8,128)S(1)} %collective-permute-done.4) | non-fusion elementwise | flops 393216 | bytes 4718592 | tf_op jit(solution)/shard_map/add | solution.py:455
  81.9 0.0 copy-start.2
  81.9 1.1 copy-done.2
  83.0 0.1 slice_bitcast_fusion
  83.1 2.3 %collective-permute-start.7 = (f32[4,3,16,512]{3,2,1,0:T(8,128)S(1)}, f32[4,3,16,512]{3,2,1,0:T(8,128)}, u32[]{:S(2)}, u32[]{:S(2)}) collective-permute-start(f32[4,3,16,512]{3,2,1,0:T(8,128)S(1)} %get-tuple-element.42), channel_id=1, source_target_pairs={{0,6},{1,7},{2,0},{3,1},{4,2},{5,3},{6,4},{7,5},{8,14},{9,15},{10,... | collective-permute-start | bytes 1179656 | tf_op jit(solution)/shard_map/ppermute | solution.py:338
  85.5 1.3 collective-permute-start.5
  86.7 1.2 iota_compare_fusion.1
  88.0 1.1 fusion.8
  89.1 13.0 %collective-permute-done.7 = f32[4,3,16,512]{3,2,1,0:T(8,128)} collective-permute-done((f32[4,3,16,512]{3,2,1,0:T(8,128)S(1)}, f32[4,3,16,512]{3,2,1,0:T(8,128)}, u32[]{:S(2)}, u32[]{:S(2)}) %collective-permute-start.7) | collective-permute-done | bytes 393248 | tf_op jit(solution)/shard_map/ppermute | solution.py:338
  102.1 3.3 %collective-permute-done.6 = f32[4,3,16,512]{3,2,1,0:T(8,128)} collective-permute-done((f32[4,3,16,512]{3,2,1,0:T(8,128)S(1)}, f32[4,3,16,512]{3,2,1,0:T(8,128)}, u32[]{:S(2)}, u32[]{:S(2)}) %collective-permute-start.6) | collective-permute-done | bytes 393248 | tf_op jit(solution)/shard_map/ppermute | solution.py:338
  105.5 1.5 fusion.1
  107.0 3.3 %select_add_fusion = f32[2,512,512]{2,1,0:T(8,128)} fusion(f32[2,512,512]{2,1,0:T(8,128)} %collective-permute-done.8, f32[2,512,512]{2,1,0:T(8,128)S(1)} %copy-done.1, pred[512]{0:T(512)(128)(4,1)S(1)} %get-tuple-element.54, pred[512]{0:T(512)(128)(4,1)S(1)} %get-tuple-element.55, pred[512]{0:T(512)(128)(4,1)S(1)} %get-tuple-element.53, ...), kind=kLoop, calls=%fused_computation.1 | loop fusion | flops 2621440 | bytes 6293504 | tf_op jit(solution)/shard_map/add | solution.py:452
  110.3 2.0 %collective-permute-start.21 = (f32[2,512,512]{2,1,0:T(8,128)}, f32[2,512,512]{2,1,0:T(8,128)}, u32[]{:S(2)}, u32[]{:S(2)}) collective-permute-start(f32[2,512,512]{2,1,0:T(8,128)} %select_add_fusion), channel_id=1, source_target_pairs={{0,1},{1,2},{2,3},{3,4},{4,5},{5,6},{6,7},{8,9},{9,10},{10,11},{11... | collective-permute-start | bytes 6291464 | tf_op jit(solution)/shard_map/ppermute | solution.py:338
  112.4 2.1 %collective-permute-start.11 = (f32[3,16,512]{2,1,0:T(8,128)S(1)}, f32[3,16,512]{2,1,0:T(8,128)S(1)}, u32[]{:S(2)}, u32[]{:S(2)}) collective-permute-start(f32[3,16,512]{2,1,0:T(8,128)S(1)} %get-tuple-element.45), channel_id=1, source_target_pairs={{0,96},{8,104},{16,112},{24,120},{32,0},{40,8},{48,16},{56,24},{64... | collective-permute-start | bytes 294920 | tf_op jit(solution)/shard_map/ppermute | solution.py:338
  114.5 1.5 collective-permute-start.9
  116.0 0.1 collective-permute-done.11
  116.1 4.1 %collective-permute-done.10 = f32[3,16,512]{2,1,0:T(8,128)S(1)} collective-permute-done((f32[3,16,512]{2,1,0:T(8,128)S(1)}, f32[3,16,512]{2,1,0:T(8,128)S(1)}, u32[]{:S(2)}, u32[]{:S(2)}) %collective-permute-start.10) | collective-permute-done | bytes 98336 | tf_op jit(solution)/shard_map/ppermute | solution.py:338
  120.2 0.1 collective-permute-start.14
  120.3 1.5 collective-permute-start.13
  121.8 0.5 collective-permute-start.12
  122.3 1.5 collective-permute-done.14
  123.8 1.3 collective-permute-done.13
  125.1 1.7 %collective-permute-done.12 = f32[3,16,512]{2,1,0:T(8,128)S(1)} collective-permute-done((f32[3,16,512]{2,1,0:T(8,128)S(1)}, f32[3,16,512]{2,1,0:T(8,128)S(1)}, u32[]{:S(2)}, u32[]{:S(2)}) %collective-permute-start.12) | collective-permute-done | bytes 98336 | tf_op jit(solution)/shard_map/ppermute | solution.py:338
  126.8 0.9 fusion.3
  127.7 2.0 %collective-permute-start.17 = (f32[2,16,512]{2,1,0:T(8,128)S(1)}, f32[2,16,512]{2,1,0:T(8,128)S(1)}, u32[]{:S(2)}, u32[]{:S(2)}) collective-permute-start(f32[2,16,512]{2,1,0:T(8,128)S(1)} %fusion.3), channel_id=1, source_target_pairs={{0,96},{8,104},{16,112},{24,120},{32,0},{40,8},{48,16},{56,24},{64... | collective-permute-start | bytes 196616 | tf_op jit(solution)/shard_map/ppermute | solution.py:338
  129.7 0.3 collective-permute-start.16
  130.0 0.4 collective-permute-start.15
  130.4 0.6 iota_compare_fusion
  131.0 0.6 collective-permute-done.17
  131.7 2.8 %collective-permute-done.16 = f32[2,16,512]{2,1,0:T(8,128)S(1)} collective-permute-done((f32[2,16,512]{2,1,0:T(8,128)S(1)}, f32[2,16,512]{2,1,0:T(8,128)S(1)}, u32[]{:S(2)}, u32[]{:S(2)}) %collective-permute-start.16) | collective-permute-done | bytes 65568 | tf_op jit(solution)/shard_map/ppermute | solution.py:338
  134.5 0.6 collective-permute-done.15
  135.1 0.3 collective-permute-start.20
  135.3 4.4 %collective-permute-start.19 = (f32[4,2,16,512]{3,2,1,0:T(8,128)S(1)}, f32[4,2,16,512]{3,2,1,0:T(8,128)S(1)}, u32[]{:S(2)}, u32[]{:S(2)}) collective-permute-start(f32[4,2,16,512]{3,2,1,0:T(8,128)S(1)} %pad_maximum_fusion.1.refs_0_), channel_id=1, source_target_pairs={{0,4},{1,5},{2,6},{3,7},{4,0},{5,1},{6,2},{7,3},{8,12},{9,13},{10,... | collective-permute-start | bytes 786440 | tf_op jit(solution)/shard_map/ppermute | solution.py:338
  139.7 4.7 %add_add_fusion = f32[2,512,512]{2,1,0:T(8,128)} fusion(f32[2,512,512]{2,1,0:T(8,128)} %collective-permute-done.21, f32[2,512,512]{2,1,0:T(8,128)S(1)} %copy-done, f32[2,512,512]{2,1,0:T(8,128)} %collective-permute-done.8, f32[2,512,512]{2,1,0:T(8,128)} %get-tuple-element.34, pred[512]{0:T(512)(128)(4,1)S(1)} %iota_compare_fusion.5, ...), kind=kLoop, calls=%fused_computation | loop fusion | flops 3670016 | bytes 10487808 | tf_op jit(solution)/shard_map/add | solution.py:469
  144.5 3.6 %collective-permute-done.18.refs_1_ = f32[4,2,16,512]{3,2,1,0:T(8,128)S(1)} collective-permute-done((f32[4,2,16,512]{3,2,1,0:T(8,128)S(1)}, f32[4,2,16,512]{3,2,1,0:T(8,128)S(1)}, u32[]{:S(2)}, u32[]{:S(2)}) %collective-permute-start.18) | collective-permute-done | bytes 262176 | tf_op jit(solution)/shard_map/ppermute | solution.py:338
  148.0 0.1 pad_maximum_fusion
  148.2 4.6 %collective-permute-start.22 = (f32[4,4,2,16,512]{4,3,2,1,0:T(8,128)S(1)}, f32[4,4,2,16,512]{4,3,2,1,0:T(8,128)S(1)}, u32[]{:S(2)}, u32[]{:S(2)}) collective-permute-start(f32[4,4,2,16,512]{4,3,2,1,0:T(8,128)S(1)} %pad_maximum_fusion), channel_id=1, source_target_pairs={{0,1},{1,0},{2,3},{3,2},{4,5},{5,4},{6,7},{7,6},{8,9},{9,8},{10,11... | collective-permute-start | bytes 3145736 | tf_op jit(solution)/shard_map/ppermute | solution.py:338
  152.8 2.3 %place_mine.1.refs_1_ = f32[2,512,512]{2,1,0:T(8,128)} custom-call(f32[4,2,16,512]{3,2,1,0:T(8,128)} %copy-done.3, f32[4,2,16,512]{3,2,1,0:T(8,128)} %copy-done.8, f32[4,2,16,512]{3,2,1,0:T(8,128)} %copy-done.7, f32[4,2,16,512]{3,2,1,0:T(8,128)} %copy-done.6), custom_call_target="tpu_custom_call" | custom-call | bytes 2097152 | tf_op jit(solution)/shard_map/place_mine/pallas_call | solution.py:402
  155.0 0.0 collective-permute-done.22.refs_0_
  155.1 1.0 copy-done.5
  156.1 2.3 %place_other.1 = f32[2,512,512]{2,1,0:T(8,128)} custom-call(f32[4,4,2,16,512]{4,3,2,1,0:T(8,128)} %copy-done.5, f32[2,512,512]{2,1,0:T(8,128)} %place_mine.1.refs_1_), custom_call_target="tpu_custom_call", output_to_operand_aliasing={{}: (1, {})} | custom-call | bytes 2097152 | tf_op jit(solution)/shard_map/place_other/pallas_call | solution.py:402
  (33 shorter events, 0.2 us)
Async XLA Ops:
  3.2 20.6 %collective-permute-start = (f32[2,320,512]{2,1,0:T(8,128)S(1)}, f32[2,320,512]{2,1,0:T(8,128)S(1)}, u32[]{:S(2)}, u32[]{:S(2)}) collective-permute-start(f32[2,320,512]{2,1,0:T(8,128)S(1)} %slice.42), channel_id=1, source_target_pairs={{1,0},{2,1},{3,2},{4,3},{5,4},{6,5},{7,6},{9,8},{10,9},{11,10},{12... | collective-permute-start | bytes 3932168 | tf_op jit(solution)/shard_map/ppermute | solution.py:338
  12.6 9.0 %copy-start.9 = (s32[16,2]{0,1:T(2,128)S(1)}, s32[16,2]{0,1:T(2,128)}, u32[]{:S(2)}) copy-start(s32[16,2]{0,1:T(2,128)} %param.12) | copy-start | bytes 388
  12.6 27.6 %all-to-all-start = ((f32[16,32,512]{2,1,0:T(8,128)}), f32[16,32,512]{2,1,0:T(8,128)}, u32[]{:S(2)}, u32[]{:S(2)}) async-start(f32[16,32,512]{2,1,0:T(8,128)} %bin_frames.1), calls=%async_computation | async-start | bytes 2097152 | tf_op jit(solution)/shard_map/all_to_all | solution.py:435
  19.6 13.8 %collective-permute-start.1 = (f32[2,192,512]{2,1,0:T(8,128)S(1)}, f32[2,192,512]{2,1,0:T(8,128)}, u32[]{:S(2)}, u32[]{:S(2)}) collective-permute-start(f32[2,192,512]{2,1,0:T(8,128)S(1)} %slice.43), channel_id=1, source_target_pairs={{1,0},{2,1},{3,2},{4,3},{5,4},{6,5},{7,6},{9,8},{10,9},{11,10},{12... | collective-permute-start | bytes 2359304 | tf_op jit(solution)/shard_map/ppermute | solution.py:338
  23.9 17.6 %copy-start.4 = (f32[2,320,512]{2,1,0:T(8,128)}, f32[2,320,512]{2,1,0:T(8,128)S(1)}, u32[]{:S(2)}) copy-start(f32[2,320,512]{2,1,0:T(8,128)S(1)} %collective-permute-done.r0_hbm) | copy-start | bytes 3932164
  25.4 34.2 %collective-permute-start.2 = (f32[2,320,512]{2,1,0:T(8,128)}, f32[2,320,512]{2,1,0:T(8,128)}, u32[]{:S(2)}, u32[]{:S(2)}) collective-permute-start(f32[2,320,512]{2,1,0:T(8,128)} %broadcast_select_fusion), channel_id=1, source_target_pairs={{1,9},{3,11},{5,13},{7,15},{8,0},{9,17},{10,2},{11,19},{12,4},{13,... | collective-permute-start | bytes 3932168 | tf_op jit(solution)/shard_map/ppermute | solution.py:338
  41.4 18.1 %collective-permute-start.3 = (f32[2,192,512]{2,1,0:T(8,128)S(1)}, f32[2,192,512]{2,1,0:T(8,128)S(1)}, u32[]{:S(2)}, u32[]{:S(2)}) collective-permute-start(f32[2,192,512]{2,1,0:T(8,128)S(1)} %broadcast_select_fusion.1), channel_id=1, source_target_pairs={{1,9},{3,11},{5,13},{7,15},{8,0},{9,17},{10,2},{11,19},{12,4},{13,... | collective-permute-start | bytes 2359304 | tf_op jit(solution)/shard_map/ppermute | solution.py:338
  59.6 1.0 copy-start.10
  75.0 5.1 %collective-permute-start.4 = (f32[4,4,3,16,512]{4,3,2,1,0:T(8,128)}, f32[4,4,3,16,512]{4,3,2,1,0:T(8,128)S(1)}, u32[]{:S(2)}, u32[]{:S(2)}) collective-permute-start(f32[4,4,3,16,512]{4,3,2,1,0:T(8,128)} %get-tuple-element.29), channel_id=1, source_target_pairs={{0,1},{1,0},{2,3},{3,2},{4,5},{5,4},{6,7},{7,6},{8,9},{9,8},{10,11... | collective-permute-start | bytes 4718600 | tf_op jit(solution)/shard_map/ppermute | solution.py:338
  75.1 31.9 %collective-permute-start.8 = (f32[2,512,512]{2,1,0:T(8,128)}, f32[2,512,512]{2,1,0:T(8,128)}, u32[]{:S(2)}, u32[]{:S(2)}) collective-permute-start(f32[2,512,512]{2,1,0:T(8,128)} %get-tuple-element.34), channel_id=1, source_target_pairs={{0,8},{1,121},{2,10},{3,123},{4,12},{5,125},{6,14},{7,127},{8,16},... | collective-permute-start | bytes 6291464 | tf_op jit(solution)/shard_map/ppermute | solution.py:338
  81.9 1.1 copy-start.2
  83.0 24.0 %copy-start.1 = (f32[2,512,512]{2,1,0:T(8,128)S(1)}, f32[2,512,512]{2,1,0:T(8,128)}, u32[]{:S(2)}) copy-start(f32[2,512,512]{2,1,0:T(8,128)} %get-tuple-element.34) | copy-start | bytes 6291460
  83.1 19.0 %collective-permute-start.7 = (f32[4,3,16,512]{3,2,1,0:T(8,128)S(1)}, f32[4,3,16,512]{3,2,1,0:T(8,128)}, u32[]{:S(2)}, u32[]{:S(2)}) collective-permute-start(f32[4,3,16,512]{3,2,1,0:T(8,128)S(1)} %get-tuple-element.42), channel_id=1, source_target_pairs={{0,6},{1,7},{2,0},{3,1},{4,2},{5,3},{6,4},{7,5},{8,14},{9,15},{10,... | collective-permute-start | bytes 1179656 | tf_op jit(solution)/shard_map/ppermute | solution.py:338
  85.4 20.0 %collective-permute-start.6 = (f32[4,3,16,512]{3,2,1,0:T(8,128)S(1)}, f32[4,3,16,512]{3,2,1,0:T(8,128)}, u32[]{:S(2)}, u32[]{:S(2)}) collective-permute-start(f32[4,3,16,512]{3,2,1,0:T(8,128)S(1)} %get-tuple-element.43), channel_id=1, source_target_pairs={{0,2},{1,3},{2,4},{3,5},{4,6},{5,7},{6,0},{7,1},{8,10},{9,11},{10,... | collective-permute-start | bytes 1179656 | tf_op jit(solution)/shard_map/ppermute | solution.py:338
  85.5 20.0 %collective-permute-start.5 = (f32[4,3,16,512]{3,2,1,0:T(8,128)S(1)}, f32[4,3,16,512]{3,2,1,0:T(8,128)}, u32[]{:S(2)}, u32[]{:S(2)}) collective-permute-start(f32[4,3,16,512]{3,2,1,0:T(8,128)S(1)} %get-tuple-element.44), channel_id=1, source_target_pairs={{0,4},{1,5},{2,6},{3,7},{4,0},{5,1},{6,2},{7,3},{8,12},{9,13},{10,... | collective-permute-start | bytes 1179656 | tf_op jit(solution)/shard_map/ppermute | solution.py:338
  110.3 29.4 %copy-start = (f32[2,512,512]{2,1,0:T(8,128)S(1)}, f32[2,512,512]{2,1,0:T(8,128)}, u32[]{:S(2)}) copy-start(f32[2,512,512]{2,1,0:T(8,128)} %tile_hbm.1) | copy-start | bytes 6291460
  110.3 29.4 %collective-permute-start.21 = (f32[2,512,512]{2,1,0:T(8,128)}, f32[2,512,512]{2,1,0:T(8,128)}, u32[]{:S(2)}, u32[]{:S(2)}) collective-permute-start(f32[2,512,512]{2,1,0:T(8,128)} %select_add_fusion), channel_id=1, source_target_pairs={{0,1},{1,2},{2,3},{3,4},{4,5},{5,6},{6,7},{8,9},{9,10},{10,11},{11... | collective-permute-start | bytes 6291464 | tf_op jit(solution)/shard_map/ppermute | solution.py:338
  112.4 3.7 %collective-permute-start.11 = (f32[3,16,512]{2,1,0:T(8,128)S(1)}, f32[3,16,512]{2,1,0:T(8,128)S(1)}, u32[]{:S(2)}, u32[]{:S(2)}) collective-permute-start(f32[3,16,512]{2,1,0:T(8,128)S(1)} %get-tuple-element.45), channel_id=1, source_target_pairs={{0,96},{8,104},{16,112},{24,120},{32,0},{40,8},{48,16},{56,24},{64... | collective-permute-start | bytes 294920 | tf_op jit(solution)/shard_map/ppermute | solution.py:338
  114.5 5.7 %collective-permute-start.10 = (f32[3,16,512]{2,1,0:T(8,128)S(1)}, f32[3,16,512]{2,1,0:T(8,128)S(1)}, u32[]{:S(2)}, u32[]{:S(2)}) collective-permute-start(f32[3,16,512]{2,1,0:T(8,128)S(1)} %get-tuple-element.46), channel_id=1, source_target_pairs={{0,32},{8,40},{16,48},{24,56},{32,64},{40,72},{48,80},{56,88},{64,... | collective-permute-start | bytes 294920 | tf_op jit(solution)/shard_map/ppermute | solution.py:338
  114.5 5.7 %collective-permute-start.9 = (f32[3,16,512]{2,1,0:T(8,128)S(1)}, f32[3,16,512]{2,1,0:T(8,128)S(1)}, u32[]{:S(2)}, u32[]{:S(2)}) collective-permute-start(f32[3,16,512]{2,1,0:T(8,128)S(1)} %get-tuple-element.47), channel_id=1, source_target_pairs={{0,64},{8,72},{16,80},{24,88},{32,96},{40,104},{48,112},{56,120},{... | collective-permute-start | bytes 294920 | tf_op jit(solution)/shard_map/ppermute | solution.py:338
  120.2 3.5 %collective-permute-start.14 = (f32[3,16,512]{2,1,0:T(8,128)S(1)}, f32[3,16,512]{2,1,0:T(8,128)S(1)}, u32[]{:S(2)}, u32[]{:S(2)}) collective-permute-start(f32[3,16,512]{2,1,0:T(8,128)S(1)} %fusion.2), channel_id=1, source_target_pairs={{0,24},{8,0},{16,8},{24,16},{32,56},{40,32},{48,40},{56,48},{64,88... | collective-permute-start | bytes 294920 | tf_op jit(solution)/shard_map/ppermute | solution.py:338
  120.3 4.7 %collective-permute-start.13 = (f32[3,16,512]{2,1,0:T(8,128)S(1)}, f32[3,16,512]{2,1,0:T(8,128)S(1)}, u32[]{:S(2)}, u32[]{:S(2)}) collective-permute-start(f32[3,16,512]{2,1,0:T(8,128)S(1)} %fusion.2), channel_id=1, source_target_pairs={{0,8},{8,16},{16,24},{24,0},{32,40},{40,48},{48,56},{56,32},{64,72... | collective-permute-start | bytes 294920 | tf_op jit(solution)/shard_map/ppermute | solution.py:338
  121.8 5.0 %collective-permute-start.12 = (f32[3,16,512]{2,1,0:T(8,128)S(1)}, f32[3,16,512]{2,1,0:T(8,128)S(1)}, u32[]{:S(2)}, u32[]{:S(2)}) collective-permute-start(f32[3,16,512]{2,1,0:T(8,128)S(1)} %fusion.2), channel_id=1, source_target_pairs={{0,16},{8,24},{16,0},{24,8},{32,48},{40,56},{48,32},{56,40},{64,80... | collective-permute-start | bytes 294920 | tf_op jit(solution)/shard_map/ppermute | solution.py:338
  127.7 4.0 %collective-permute-start.17 = (f32[2,16,512]{2,1,0:T(8,128)S(1)}, f32[2,16,512]{2,1,0:T(8,128)S(1)}, u32[]{:S(2)}, u32[]{:S(2)}) collective-permute-start(f32[2,16,512]{2,1,0:T(8,128)S(1)} %fusion.3), channel_id=1, source_target_pairs={{0,96},{8,104},{16,112},{24,120},{32,0},{40,8},{48,16},{56,24},{64... | collective-permute-start | bytes 196616 | tf_op jit(solution)/shard_map/ppermute | solution.py:338
  129.7 4.7 %collective-permute-start.16 = (f32[2,16,512]{2,1,0:T(8,128)S(1)}, f32[2,16,512]{2,1,0:T(8,128)S(1)}, u32[]{:S(2)}, u32[]{:S(2)}) collective-permute-start(f32[2,16,512]{2,1,0:T(8,128)S(1)} %fusion.3), channel_id=1, source_target_pairs={{0,64},{8,72},{16,80},{24,88},{32,96},{40,104},{48,112},{56,120},{... | collective-permute-start | bytes 196616 | tf_op jit(solution)/shard_map/ppermute | solution.py:338
  130.0 5.0 %collective-permute-start.15 = (f32[2,16,512]{2,1,0:T(8,128)S(1)}, f32[2,16,512]{2,1,0:T(8,128)S(1)}, u32[]{:S(2)}, u32[]{:S(2)}) collective-permute-start(f32[2,16,512]{2,1,0:T(8,128)S(1)} %fusion.3), channel_id=1, source_target_pairs={{0,32},{8,40},{16,48},{24,56},{32,64},{40,72},{48,80},{56,88},{64,... | collective-permute-start | bytes 196616 | tf_op jit(solution)/shard_map/ppermute | solution.py:338
  135.1 13.0 %copy-start.3 = (f32[4,2,16,512]{3,2,1,0:T(8,128)}, f32[4,2,16,512]{3,2,1,0:T(8,128)S(1)}, u32[]{:S(2)}) copy-start(f32[4,2,16,512]{3,2,1,0:T(8,128)S(1)} %pad_maximum_fusion.1.refs_0_) | copy-start | bytes 786436
  135.1 9.4 %collective-permute-start.20 = (f32[4,2,16,512]{3,2,1,0:T(8,128)S(1)}, f32[4,2,16,512]{3,2,1,0:T(8,128)S(1)}, u32[]{:S(2)}, u32[]{:S(2)}) collective-permute-start(f32[4,2,16,512]{3,2,1,0:T(8,128)S(1)} %pad_maximum_fusion.1.refs_0_), channel_id=1, source_target_pairs={{0,6},{1,7},{2,0},{3,1},{4,2},{5,3},{6,4},{7,5},{8,14},{9,15},{10,... | collective-permute-start | bytes 786440 | tf_op jit(solution)/shard_map/ppermute | solution.py:338
  135.3 9.1 %collective-permute-start.19 = (f32[4,2,16,512]{3,2,1,0:T(8,128)S(1)}, f32[4,2,16,512]{3,2,1,0:T(8,128)S(1)}, u32[]{:S(2)}, u32[]{:S(2)}) collective-permute-start(f32[4,2,16,512]{3,2,1,0:T(8,128)S(1)} %pad_maximum_fusion.1.refs_0_), channel_id=1, source_target_pairs={{0,4},{1,5},{2,6},{3,7},{4,0},{5,1},{6,2},{7,3},{8,12},{9,13},{10,... | collective-permute-start | bytes 786440 | tf_op jit(solution)/shard_map/ppermute | solution.py:338
  139.7 8.3 %collective-permute-start.18 = (f32[4,2,16,512]{3,2,1,0:T(8,128)S(1)}, f32[4,2,16,512]{3,2,1,0:T(8,128)S(1)}, u32[]{:S(2)}, u32[]{:S(2)}) collective-permute-start(f32[4,2,16,512]{3,2,1,0:T(8,128)S(1)} %pad_maximum_fusion.1.refs_0_), channel_id=1, source_target_pairs={{0,2},{1,3},{2,4},{3,5},{4,6},{5,7},{6,0},{7,1},{8,10},{9,11},{10,... | collective-permute-start | bytes 786440 | tf_op jit(solution)/shard_map/ppermute | solution.py:338
  144.5 8.3 %copy-start.6 = (f32[4,2,16,512]{3,2,1,0:T(8,128)}, f32[4,2,16,512]{3,2,1,0:T(8,128)S(1)}, u32[]{:S(2)}) copy-start(f32[4,2,16,512]{3,2,1,0:T(8,128)S(1)} %collective-permute-done.20.refs_3_) | copy-start | bytes 786436
  144.5 8.3 %copy-start.7 = (f32[4,2,16,512]{3,2,1,0:T(8,128)}, f32[4,2,16,512]{3,2,1,0:T(8,128)S(1)}, u32[]{:S(2)}) copy-start(f32[4,2,16,512]{3,2,1,0:T(8,128)S(1)} %collective-permute-done.19.refs_2_) | copy-start | bytes 786436
  148.0 4.7 %copy-start.8 = (f32[4,2,16,512]{3,2,1,0:T(8,128)}, f32[4,2,16,512]{3,2,1,0:T(8,128)S(1)}, u32[]{:S(2)}) copy-start(f32[4,2,16,512]{3,2,1,0:T(8,128)S(1)} %collective-permute-done.18.refs_1_) | copy-start | bytes 786436
  148.2 6.9 %collective-permute-start.22 = (f32[4,4,2,16,512]{4,3,2,1,0:T(8,128)S(1)}, f32[4,4,2,16,512]{4,3,2,1,0:T(8,128)S(1)}, u32[]{:S(2)}, u32[]{:S(2)}) collective-permute-start(f32[4,4,2,16,512]{4,3,2,1,0:T(8,128)S(1)} %pad_maximum_fusion), channel_id=1, source_target_pairs={{0,1},{1,0},{2,3},{3,2},{4,5},{5,4},{6,7},{7,6},{8,9},{9,8},{10,11... | collective-permute-start | bytes 3145736 | tf_op jit(solution)/shard_map/ppermute | solution.py:338
  155.1 1.0 copy-start.5
